TPU v7x, 256 devices: a whole 4x4x8 slice. The times are simulated.
256 devices in a mesh: docs: 128 (over x, y, z), rep: 2 (over core).
Axes of the slice: x: 4, y: 4, z: 8, core: 2. Of those that a mesh axis runs over, the one named last changes fastest.
Arguments:
- slab: bfloat16 [131072, 768], P(('docs', 'rep')), may hold values from -9 to 9
- old_cluster: int32 [131072, 1], P(('docs', 'rep')), may hold values from 0 to 127; in each aligned block of 512 rows (0 to 511, 512 to 1023, ...) at most 8 rows name the same one
- new_cluster: int32 [131072, 1], P(('docs', 'rep')), may hold values from 0 to 127; in each aligned block of 512 rows (0 to 511, 512 to 1023, ...) at most 8 rows name the same one
- anchor_ids: int32 [128, 1536], P('docs', 'rep'), may hold values from 0 to 511
- anchor_new: bfloat16 [128, 1536, 768], P('docs', 'rep'), may hold values from -9 to 9
- owner_table: int32 [128], replicated, may hold values from 0 to 127, each once
Outputs:
- relayed: bfloat16 [128, 2048, 768], P('docs', 'rep')
Inputs may be any that keep to these rules, and one draw needn't show every extreme that they name: `old_cluster`: the 512 documents of one device name each cluster at most 8 times. `new_cluster`: the 512 documents of one device name each new cluster at most 8 times. `owner_table`: every docs index owns exactly one new cluster.
All inputs are finite; a program needn't handle non-finite values.
Results may differ from a plain program's by a relative error of at most 0.022.
Values may be sent and summed in bfloat16 or wider, within the bound.
No kernel may reach another device: no remote copies, remote signals or barrier semaphores. Data moves between devices by JAX's collectives and lax.ppermute only.
A program may use at most 64 MiB of HBM per device.

v0:
```python
import math

import jax
import jax.numpy as jnp
from jax import lax
from jax.sharding import PartitionSpec as P

ITERS = 3


EPS = 1e-06
polar_scale = 0.3


def slot_ranks(labels, count):
    onehot = (labels[:, None] == jnp.arange(count, dtype=jnp.int32)[None, :]).astype(jnp.int32)
    earlier = jnp.cumsum(onehot, axis=0) - onehot
    return jnp.sum(earlier * onehot, axis=1)


def newton_step(part_x, full_x):
    square = jnp.einsum("id,jd->ij", part_x, full_x, preferred_element_type=jnp.float32).astype(
        jnp.bfloat16
    )
    update = jnp.dot(square, full_x, preferred_element_type=jnp.float32)
    return (1.5 * part_x.astype(jnp.float32) - 0.5 * update).astype(jnp.bfloat16)


def shards(slab, old_cluster, new_cluster, anchor_ids, anchor_new, owner_table):
    docs_count = lax.axis_size("docs")
    row_count = slab.shape[0]
    width = slab.shape[1]
    capacity = 2 * row_count // docs_count
    half = anchor_ids.shape[1]
    per_source = half // docs_count
    asked = lax.all_to_all(
        anchor_ids.reshape(docs_count, per_source), "docs", split_axis=0, concat_axis=0, tiled=True
    )
    picked = jnp.take(slab, asked.reshape(-1), axis=0).reshape(asked.shape + (width,))
    fetched = lax.all_to_all(picked, "docs", split_axis=0, concat_axis=0, tiled=True)
    partial_gram = jnp.einsum(
        "ad,ae->de", fetched.reshape(half, width), anchor_new[0], preferred_element_type=jnp.float32
    )
    gram = lax.psum(partial_gram, "rep")
    factor = polar_scale * math.sqrt(width) * lax.rsqrt(jnp.sum(gram * gram) + EPS)
    iterate = (gram * factor).astype(jnp.bfloat16)
    for step in range(ITERS):
        iterate = newton_step(iterate, iterate)
    old_labels = old_cluster[:, 0]
    old_slot = old_labels * capacity + slot_ranks(old_labels, docs_count)
    outgoing = jnp.zeros((docs_count * capacity, width), jnp.bfloat16).at[old_slot].set(slab)
    outgoing = outgoing.reshape(docs_count, capacity, width)
    arrived = lax.all_to_all(outgoing, "docs", split_axis=0, concat_axis=0, tiled=True)
    flat = arrived.reshape(-1, width)
    moved = jnp.dot(flat, iterate, preferred_element_type=jnp.float32).astype(jnp.bfloat16)
    returned = lax.all_to_all(
        moved.reshape(arrived.shape), "docs", split_axis=0, concat_axis=0, tiled=True
    )
    mapped = jnp.take(returned.reshape(-1, width), old_slot, axis=0)
    new_labels = new_cluster[:, 0]
    matches = new_labels[:, None] == jnp.arange(owner_table.shape[0], dtype=jnp.int32)[None, :]
    owners = jnp.sum(jnp.where(matches, owner_table[None, :], 0), axis=1)
    new_slot = owners * capacity + slot_ranks(new_labels, docs_count)
    onward = jnp.zeros((docs_count * capacity, width), jnp.bfloat16).at[new_slot].set(mapped)
    onward = onward.reshape(docs_count, capacity, width)
    arrived_rows = lax.all_to_all(onward, "docs", split_axis=0, concat_axis=0, tiled=True)
    return arrived_rows.reshape(1, docs_count * capacity, width)


def solution(mesh):
    in_specs = (
        P(("docs", "rep"), None),
        P(("docs", "rep"), None),
        P(("docs", "rep"), None),
        P("docs", "rep"),
        P("docs", "rep", None),
        P(),
    )
    out_specs = P("docs", "rep", None)
    return jax.shard_map(shards, mesh=mesh, in_specs=in_specs, out_specs=out_specs, check_vma=False)
```

profile of v0, /device:TPU:32, one launch (start us, length us, event | category | flops | bytes accessed | tf_op | source)
XLA Modules:
  0.0 255.6 jit_solution(12522036333067043556)
XLA Ops:
  6.5 0.0 copy-start
  6.5 0.8 reduce.1
  7.3 0.1 all_to_all.19
  7.5 25.9 %all_to_all.29 = s32[128,1,6]{2,1,0:T(1,128)S(1)} all-to-all(s32[128,1,6]{2,1,0:T(1,128)S(1)} %bitcast.66), channel_id=1, replica_groups=mesh['docs'=128,'rep'=2] {'docs'}, dimensions={0} | all-to-all | bytes 6144 | tf_op jit(solution)/shard_map/all_to_all | solution.py:36
  33.4 0.5 broadcast.151
  33.9 0.8 reduce.8
  34.7 0.1 reshape.143
  34.9 5.2 %gather_fusion = bf16[768,768]{1,0:T(8,128)(2,1)} fusion(bf16[512,768]{1,0:T(8,128)(2,1)} %param.6, s32[1024]{0:T(1024)S(1)} %pad_clamp_fusion.1), kind=kCustom, calls=%fused_computation | custom fusion | bytes 2362368 | tf_op jit(solution)/shard_map/jit(_take)/gather | solution.py:39
  40.1 2.2 gather.11
  42.4 1.4 broadcast_select_fusion
  43.8 0.0 copy-start.2
  43.8 6.8 %all-to-all-start.2 = ((bf16[128,6,768]{2,1,0:T(8,128)(2,1)}), bf16[128,6,768]{2,1,0:T(8,128)(2,1)S(1)}, u32[]{:S(2)}, u32[]{:S(2)}) async-start(bf16[128,6,768]{2,1,0:T(8,128)(2,1)} %broadcast_select_fusion), calls=%async_computation.2 | async-start | bytes 3145728 | tf_op jit(solution)/shard_map/all_to_all | solution.py:40
  50.6 0.0 all-reduce.2.cloned.1.call-start
  50.7 0.0 copy-done.2
  50.7 0.1 copy.15
  50.8 41.4 %all-to-all-done.2 = bf16[128,6,768]{2,1,0:T(8,128)(2,1)S(1)} async-done(((bf16[128,6,768]{2,1,0:T(8,128)(2,1)}), bf16[128,6,768]{2,1,0:T(8,128)(2,1)S(1)}, u32[]{:S(2)}, u32[]{:S(2)}) %all-to-all-start.2) | async-done | bytes 1179680 | tf_op jit(solution)/shard_map/all_to_all | solution.py:40
  92.2 1.2 reshape.144
  93.4 0.0 copy-done
  93.4 3.8 %fusion.4 = f32[768,768]{1,0:T(8,128)} fusion(bf16[768,768]{1,0:T(8,128)(2,1)} %reshape.144, bf16[1,768,768]{2,1,0:T(8,128)(2,1)S(1)} %copy-done), kind=kOutput, calls=%fused_computation.16 | convolution fusion | flops 905969664 | bytes 4718592 | tf_op jit(solution)/shard_map/ad,ae->de/dot_general | solution.py:41
  97.2 0.0 all-reduce.2.cloned.1.call-update
  97.2 0.2 fusion.17
  97.5 0.2 fusion.14
  97.8 4.4 %scatter_custom_fusion = bf16[1024,768]{1,0:T(8,128)(2,1)} fusion(s32[512]{0:T(512)S(1)} %bitcast.74, bf16[512,768]{1,0:T(8,128)(2,1)} %param.6, bf16[]{:T(256)} %constant.24.clone.1), kind=kCustom, calls=%fused_computation.21 | custom fusion | bytes 1573376 | tf_op jit(solution)/shard_map/scatter | solution.py:51
  102.1 7.8 %all-to-all-start = ((bf16[128,8,768]{2,1,0:T(8,128)(2,1)}), bf16[128,8,768]{2,1,0:T(8,128)(2,1)}, u32[]{:S(2)}, u32[]{:S(2)}) async-start(bf16[128,8,768]{2,1,0:T(8,128)(2,1)} %bitcast.14), calls=%async_computation | async-start | bytes 3145728 | tf_op jit(solution)/shard_map/all_to_all | solution.py:53
  110.0 13.3 %all-reduce.2.cloned.1.call-done = f32[768,768]{1,0:T(8,128)} async-done(((f32[768,768]{1,0:T(8,128)}), f32[768,768]{1,0:T(8,128)}) %all-reduce.2.cloned.1.call-update) | async-done | bytes 2359312 | tf_op jit(solution)/shard_map/psum | solution.py:44
  123.3 0.0 copy-start.1
  123.3 3.0 %multiply_reduce_fusion = f32[]{:T(128)} fusion(f32[768,768]{1,0:T(8,128)} %all-reduce.2.cloned.1.call-done), kind=kLoop, calls=%fused_computation.8 | loop fusion | flops 1179647 | bytes 2359300 | tf_op jit(solution)/shard_map/reduce_sum | solution.py:45
  126.9 0.0 copy-done.1
  126.9 3.2 %subtract_convert_fusion.2 = bf16[768,768]{1,0:T(8,128)(2,1)} fusion(f32[768,768]{1,0:T(8,128)S(1)} %copy-done.1, f32[]{:T(128)S(6)} %mul_shard_map.3), kind=kOutput, calls=%fused_computation.6 | convolution fusion | flops 1819017216 | bytes 3538948 | tf_op jit(solution)/shard_map/dot_general | solution.py:25
  130.1 4.8 %subtract_convert_fusion.1 = bf16[768,768]{1,0:T(8,128)(2,1)S(1)} fusion(bf16[768,768]{1,0:T(8,128)(2,1)} %subtract_convert_fusion.2), kind=kOutput, calls=%fused_computation.5 | convolution fusion | flops 1815478272 | bytes 2359296 | tf_op jit(solution)/shard_map/dot_general | solution.py:25
  134.8 2.1 subtract_convert_fusion
  137.0 12.3 %all-to-all-done = bf16[128,8,768]{2,1,0:T(8,128)(2,1)} async-done(((bf16[128,8,768]{2,1,0:T(8,128)(2,1)}), bf16[128,8,768]{2,1,0:T(8,128)(2,1)}, u32[]{:S(2)}, u32[]{:S(2)}) %all-to-all-start) | async-done | bytes 1572896 | tf_op jit(solution)/shard_map/all_to_all | solution.py:53
  149.3 3.9 %fusion.1 = bf16[128,8,768]{2,1,0:T(8,128)(2,1)} fusion(bf16[768,768]{1,0:T(8,128)(2,1)S(1)} %subtract_convert_fusion, bf16[128,8,768]{2,1,0:T(8,128)(2,1)} %all-to-all-done), kind=kOutput, calls=%fused_computation.15 | convolution fusion | flops 1208745984 | bytes 4325376 | tf_op jit(solution)/shard_map/dot_general | solution.py:55
  153.2 0.0 copy-start.3
  153.2 0.0 copy-start.4
  153.2 6.8 %all-to-all-start.3 = ((bf16[128,8,768]{2,1,0:T(8,128)(2,1)}), bf16[128,8,768]{2,1,0:T(8,128)(2,1)S(1)}, u32[]{:S(2)}, u32[]{:S(2)}) async-start(bf16[128,8,768]{2,1,0:T(8,128)(2,1)} %fusion.1), calls=%async_computation.3 | async-start | bytes 3145728 | tf_op jit(solution)/shard_map/all_to_all | solution.py:56
  160.0 0.0 copy-done.3
  160.0 0.1 copy.13
  160.1 0.2 fusion.19
  160.5 0.0 copy-done.4
  160.5 0.3 select_reduce_fusion
  160.8 37.2 %all-to-all-done.3 = bf16[128,8,768]{2,1,0:T(8,128)(2,1)S(1)} async-done(((bf16[128,8,768]{2,1,0:T(8,128)(2,1)}), bf16[128,8,768]{2,1,0:T(8,128)(2,1)S(1)}, u32[]{:S(2)}, u32[]{:S(2)}) %all-to-all-start.3) | async-done | bytes 1572896 | tf_op jit(solution)/shard_map/all_to_all | solution.py:56
  197.9 6.8 %scatter_custom_fusion.1 = bf16[1024,768]{1,0:T(8,128)(2,1)} fusion(s32[512]{0:T(512)S(1)} %bitcast.77, bf16[]{:T(256)} %constant.24.clone.1, pred[512]{0:T(512)(128)(4,1)S(1)} %get-tuple-element.7, bf16[]{:T(256)} %constant.47.clone.1, bf16[1024,768]{1,0:T(8,128)(2,1)S(1)} %bitcast.58, s32[1024]{0:T(1024)S(1)} %pad_clamp_fusion), kind=kCustom, calls=%fused_computation.18 | custom fusion | flops 393216 | bytes 3150340 | tf_op jit(solution)/shard_map/scatter | solution.py:64
  204.7 42.8 %all_to_all.30 = bf16[128,8,768]{2,1,0:T(8,128)(2,1)S(1)} all-to-all(bf16[128,8,768]{2,1,0:T(8,128)(2,1)} %bitcast.59), channel_id=1, replica_groups=mesh['docs'=128,'rep'=2] {'docs'}, dimensions={0} | all-to-all | bytes 3145728 | tf_op jit(solution)/shard_map/all_to_all | solution.py:66
  247.6 1.1 copy.20
  (19 shorter events, 0.3 us)
Async XLA Ops:
  6.5 86.8 %copy-start = (bf16[1,768,768]{2,1,0:T(8,128)(2,1)S(1)}, bf16[1,768,768]{2,1,0:T(8,128)(2,1)}, u32[]{:S(2)}) copy-start(bf16[1,768,768]{2,1,0:T(8,128)(2,1)} %param.10) | copy-start | bytes 3538948
  43.8 6.8 %copy-start.2 = (s32[512,1]{0,1:T(1,128)S(1)}, s32[512,1]{0,1:T(1,128)}, u32[]{:S(2)}) copy-start(s32[512,1]{0,1:T(1,128)} %param.7) | copy-start | bytes 6148
  43.8 48.4 %all-to-all-start.2 = ((bf16[128,6,768]{2,1,0:T(8,128)(2,1)}), bf16[128,6,768]{2,1,0:T(8,128)(2,1)S(1)}, u32[]{:S(2)}, u32[]{:S(2)}) async-start(bf16[128,6,768]{2,1,0:T(8,128)(2,1)} %broadcast_select_fusion), calls=%async_computation.2 | async-start | bytes 3145728 | tf_op jit(solution)/shard_map/all_to_all | solution.py:40
  50.6 72.7 %all-reduce.2.cloned.1.call-start = ((), (), s32[]{:S(2)}) async-start(), calls=%async_computation.5 | async-start | bytes 4718592 | tf_op jit(solution)/shard_map/psum | solution.py:44
  102.1 47.1 %all-to-all-start = ((bf16[128,8,768]{2,1,0:T(8,128)(2,1)}), bf16[128,8,768]{2,1,0:T(8,128)(2,1)}, u32[]{:S(2)}, u32[]{:S(2)}) async-start(bf16[128,8,768]{2,1,0:T(8,128)(2,1)} %bitcast.14), calls=%async_computation | async-start | bytes 3145728 | tf_op jit(solution)/shard_map/all_to_all | solution.py:53
  123.3 3.6 %copy-start.1 = (f32[768,768]{1,0:T(8,128)S(1)}, f32[768,768]{1,0:T(8,128)}, u32[]{:S(2)}) copy-start(f32[768,768]{1,0:T(8,128)} %all-reduce.2.cloned.1.call-done) | copy-start | bytes 7077892
  153.2 6.8 %copy-start.3 = (s32[512,1]{0,1:T(1,128)S(1)}, s32[512,1]{0,1:T(1,128)}, u32[]{:S(2)}) copy-start(s32[512,1]{0,1:T(1,128)} %param.8) | copy-start | bytes 6148
  153.2 7.3 %copy-start.4 = (s32[128]{0:T(128)S(1)}, s32[128]{0:T(128)}, u32[]{:S(2)}) copy-start(s32[128]{0:T(128)} %param.11) | copy-start | bytes 1540
  153.2 44.7 %all-to-all-start.3 = ((bf16[128,8,768]{2,1,0:T(8,128)(2,1)}), bf16[128,8,768]{2,1,0:T(8,128)(2,1)S(1)}, u32[]{:S(2)}, u32[]{:S(2)}) async-start(bf16[128,8,768]{2,1,0:T(8,128)(2,1)} %fusion.1), calls=%async_computation.3 | async-start | bytes 3145728 | tf_op jit(solution)/shard_map/all_to_all | solution.py:56
Sparse Core Ops, SparseCore 0:
  97.3 25.9 all-reduce.1
where the time goes:
time: 256 us
  waiting for transfers between devices  104 us (41%)
  blocking collectives  68.8 us (27%)
  starting transfers between devices  21.4 us (8%)
  matrix products  17.8 us (7%)
  local copies, waits for them, and re-layouts  15.3 us (6%)
  between operations  14.2 us (6%)
  other arithmetic  14 us (5%)
    all_to_all x1, blocking collectives, shards(): lax.all_to_all(onward, 'docs', split_axis=0, concat_axis=0, tiled=True)  42.8 us
    all_to_all x1, waiting for transfers between devices, shards(): lax.all_to_all(picked, 'docs', split_axis=0, concat_axis=0, tiled=True)  41.4 us
    all_to_all x1, waiting for transfers between devices, shards(): lax.all_to_all(moved.reshape(arrived.shape), 'docs', split_axis=0, concat...  37.2 us
    all_to_all x1, blocking collectives, shards(): lax.all_to_all(anchor_ids.reshape(docs_count, per_source), 'docs', split_...  25.9 us
    psum x1, waiting for transfers between devices, shards(): gram = lax.psum(partial_gram, 'rep')  13.3 us
    all_to_all x1, waiting for transfers between devices, shards(): lax.all_to_all(outgoing, 'docs', split_axis=0, concat_axis=0, tiled=True)  12.3 us
    dot_general x3, matrix products, newton_step(): update = jnp.dot(square, full_x, preferred_element_type=jnp.float32)  10.1 us
    all_to_all x1, starting transfers between devices, shards(): lax.all_to_all(outgoing, 'docs', split_axis=0, concat_axis=0, tiled=True)  7.83 us
  transfers between devices with their start and end apart: 4, of which 4 were waited for; matrix products, arithmetic and copies ran while one was open for 7% of the time, Pallas kernels for 0%

commit v1 on v0

v1 whole, which is shorter than its diff:
```python
import math

import jax
import jax.numpy as jnp
from jax import lax
from jax.sharding import PartitionSpec as P

ITERS = 3


EPS = 1e-06
polar_scale = 0.3

bf16 = jnp.bfloat16
f32 = jnp.float32


def one_hot(targets, count):
    return jnp.arange(count, dtype=jnp.int32)[:, None] == targets[None, :]


def slot_ranks(labels, count):
    rows = labels.shape[0]
    onehot = (labels[:, None] == jnp.arange(count, dtype=jnp.int32)[None, :]).astype(bf16)
    order = jnp.arange(rows, dtype=jnp.int32)
    before = (order[None, :] < order[:, None]).astype(bf16)
    earlier = jnp.dot(before, onehot, preferred_element_type=f32)
    return jnp.sum(earlier * onehot.astype(f32), axis=1).astype(jnp.int32)


def select_rows(marks, rows):
    return jnp.dot(marks.astype(bf16), rows, preferred_element_type=f32).astype(bf16)


def newton_step(x):
    square = jnp.einsum("id,jd->ij", x, x, preferred_element_type=f32).astype(bf16)
    update = jnp.dot(square, x, preferred_element_type=f32)
    return (1.5 * x.astype(f32) - 0.5 * update).astype(bf16)


def shards(slab, old_cluster, new_cluster, anchor_ids, anchor_new, owner_table):
    docs_count = lax.axis_size("docs")
    row_count, width = slab.shape
    capacity = 2 * row_count // docs_count
    slots = docs_count * capacity
    half = anchor_ids.shape[1]
    per_source = half // docs_count
    asked = lax.all_to_all(
        anchor_ids.reshape(docs_count, per_source), "docs", split_axis=0, concat_axis=0, tiled=True
    ).reshape(-1)
    picked = select_rows(asked[:, None] == jnp.arange(row_count, dtype=jnp.int32)[None, :], slab)
    fetched = lax.all_to_all(
        picked.reshape(docs_count, per_source // 2, 2, width), "docs", split_axis=0, concat_axis=0, tiled=True
    )
    partial_gram = jnp.einsum(
        "ad,ae->de", fetched.reshape(half, width), anchor_new[0], preferred_element_type=f32
    )
    gram = partial_gram + lax.ppermute(partial_gram, "rep", [(0, 1), (1, 0)])
    factor = polar_scale * math.sqrt(width) * lax.rsqrt(jnp.sum(gram * gram) + EPS)
    iterate = (gram * factor).astype(bf16)
    for step in range(ITERS):
        iterate = newton_step(iterate)

    old_labels = old_cluster[:, 0]
    old_slot = old_labels * capacity + slot_ranks(old_labels, docs_count)
    outgoing = select_rows(one_hot(old_slot, slots), slab).reshape(docs_count, capacity, width)
    arrived = lax.all_to_all(outgoing, "docs", split_axis=0, concat_axis=0, tiled=True)

    new_labels = new_cluster[:, 0]
    matches = new_labels[:, None] == jnp.arange(owner_table.shape[0], dtype=jnp.int32)[None, :]
    owners = jnp.sum(jnp.where(matches, owner_table[None, :], 0), axis=1)
    new_slot = owners * capacity + slot_ranks(new_labels, docs_count)
    source = jnp.sum(jnp.where(one_hot(new_slot, slots), old_slot[None, :] + 1, 0), axis=1) - 1

    flat = arrived.reshape(-1, width)
    moved = jnp.dot(flat, iterate, preferred_element_type=f32).astype(bf16)
    returned = lax.all_to_all(
        moved.reshape(arrived.shape), "docs", split_axis=0, concat_axis=0, tiled=True
    ).reshape(-1, width)
    onward = select_rows(source[:, None] == jnp.arange(slots, dtype=jnp.int32)[None, :], returned)
    onward = onward.reshape(docs_count, capacity, width)
    arrived_rows = lax.all_to_all(onward, "docs", split_axis=0, concat_axis=0, tiled=True)
    return arrived_rows.reshape(1, slots, width)


def solution(mesh):
    in_specs = (
        P(("docs", "rep"), None),
        P(("docs", "rep"), None),
        P(("docs", "rep"), None),
        P("docs", "rep"),
        P("docs", "rep", None),
        P(),
    )
    out_specs = P("docs", "rep", None)
    return jax.shard_map(shards, mesh=mesh, in_specs=in_specs, out_specs=out_specs, check_vma=False)
```

time: 256 us -> 230 us (0.90)
  blocking collectives: 68.8 us -> 112 us
  waiting for transfers between devices: 104 us -> 69.7 us
  between operations: 14.2 us -> 0.8 us
  local copies, waits for them, and re-layouts: 15.3 us -> 3.69 us
  other arithmetic: 14 us -> 6.21 us
  starting transfers between devices: 21.4 us -> 14.4 us
  matrix products: 17.8 us -> 23.5 us
    all_to_all x1 -> x0, waiting for transfers between devices: 41.4 us -> none  [shards(): lax.all_to_all(picked, 'docs', split_axis=0, concat_axis=0, tiled=True)]
    all_to_all x0 -> x1, blocking collectives: none -> 39.1 us  [shards(): lax.all_to_all(picked.reshape(docs_count, per_source // 2, 2, width), 'do...]
    all_to_all x1, waiting for transfers between devices: 12.3 us -> 28.1 us  [shards(): lax.all_to_all(outgoing, 'docs', split_axis=0, concat_axis=0, tiled=True)]
    psum x1 -> x0, waiting for transfers between devices: 13.3 us -> none  [shards(): gram = lax.psum(partial_gram, 'rep')]
    gather x2 -> x0, local copies, waits for them, and re-layouts: 7.44 us -> none  [shards(): jnp.take(slab, asked.reshape(-1), axis=0).reshape(asked.shape + (width,))]
    dot_general x4 -> x9, matrix products: 14 us -> 21.1 us  [the longest x3 10.4 us: newton_step(): update = jnp.dot(square, x, preferred_element_type=f32)]
    scatter x1 -> x0, other arithmetic: 6.79 us -> none  [shards(): jnp.zeros((docs_count * capacity, width), jnp.bfloat16).at[new_slot]]
    all_to_all x1 -> x0, starting transfers between devices: 6.78 us -> none  [shards(): lax.all_to_all(picked, 'docs', split_axis=0, concat_axis=0, tiled=True)]
  transfers between devices with their start and end apart: 4 -> 3, of which waited for: 4 -> 2; matrix products, arithmetic and copies ran while one was open for 7% -> 8% of each run, Pallas kernels for 0% -> 0%
where the time goes in v1:
time: 230 us
  blocking collectives  112 us (49%)
  waiting for transfers between devices  69.7 us (30%)
  matrix products  23.5 us (10%)
  starting transfers between devices  14.4 us (6%)
  other arithmetic  6.21 us (3%)
  local copies, waits for them, and re-layouts  3.69 us (2%)
    all_to_all x1, blocking collectives, shards(): lax.all_to_all(onward, 'docs', split_axis=0, concat_axis=0, tiled=True)  46.5 us
    all_to_all x1, waiting for transfers between devices, shards(): lax.all_to_all(moved.reshape(arrived.shape), 'docs', split_axis=0, concat...  41.6 us
    all_to_all x1, blocking collectives, shards(): lax.all_to_all(picked.reshape(docs_count, per_source // 2, 2, width), 'do...  39.1 us
    all_to_all x1, waiting for transfers between devices, shards(): lax.all_to_all(outgoing, 'docs', split_axis=0, concat_axis=0, tiled=True)  28.1 us
    all_to_all x1, blocking collectives, shards(): lax.all_to_all(anchor_ids.reshape(docs_count, per_source), 'docs', split_...  25.9 us
    dot_general x3, matrix products, newton_step(): update = jnp.dot(square, x, preferred_element_type=f32)  10.4 us
    all_to_all x1, starting transfers between devices, shards(): lax.all_to_all(outgoing, 'docs', split_axis=0, concat_axis=0, tiled=True)  7.67 us
    all_to_all x1, starting transfers between devices, shards(): lax.all_to_all(moved.reshape(arrived.shape), 'docs', split_axis=0, concat...  6.65 us
  transfers between devices with their start and end apart: 3, of which 2 were waited for; matrix products, arithmetic and copies ran while one was open for 8% of the time, Pallas kernels for 0%

profile of v1, /device:TPU:32, one launch (start us, length us, event | category | flops | bytes accessed | tf_op | source)
XLA Modules:
  0.0 229.9 jit_solution(10429556800582470311)
XLA Ops:
  0.0 0.0 copy-start
  0.0 0.8 reduce
  0.8 0.1 all_to_all.19
  0.9 25.9 %all_to_all.29 = s32[128,1,6]{2,1,0:T(1,128)S(1)} all-to-all(s32[128,1,6]{2,1,0:T(1,128)S(1)} %bitcast.34), channel_id=1, replica_groups=mesh['docs'=128,'rep'=2] {'docs'}, dimensions={0} | all-to-all | bytes 6144 | tf_op jit(solution)/shard_map/all_to_all | solution.py:48
  26.9 0.5 broadcast.50
  27.4 0.8 reduce.4
  28.2 0.1 eq.105
  28.3 2.0 fusion.8
  30.3 0.5 reshape.59
  30.8 39.1 %all_to_all.30 = bf16[128,3,2,768]{3,2,1,0:T(2,128)(2,1)S(1)} all-to-all(bf16[128,3,2,768]{3,2,1,0:T(2,128)(2,1)S(1)} %reshape.59), channel_id=1, replica_groups=mesh['docs'=128,'rep'=2] {'docs'}, dimensions={0} | all-to-all | bytes 2359296 | tf_op jit(solution)/shard_map/all_to_all | solution.py:52
  70.0 1.3 reshape.60
  71.2 0.0 copy-done
  71.2 0.0 copy-start.2
  71.2 0.0 copy-start.3
  71.2 0.0 copy-start.1
  71.2 0.0 copy-start.4
  71.3 2.5 %fusion.16 = f32[768,768]{1,0:T(8,128)S(1)} fusion(bf16[768,768]{1,0:T(8,128)(2,1)} %reshape.60, bf16[1,768,768]{2,1,0:T(8,128)(2,1)S(1)} %copy-done), kind=kOutput, calls=%fused_computation.26 | convolution fusion | flops 905969664 | bytes 4718592 | tf_op jit(solution)/shard_map/ad,ae->de/dot_general | solution.py:55
  73.7 0.1 collective-permute-start
  73.8 0.0 copy-done.2
  73.8 0.0 copy-done.3
  73.8 0.1 select_reduce_fusion.1
  74.0 0.3 fusion.18
  74.3 0.0 copy-done.1
  74.3 0.3 fusion.19
  74.6 0.0 copy-done.4
  74.6 2.2 fusion.9
  76.8 7.7 %all-to-all-start = ((bf16[128,8,768]{2,1,0:T(8,128)(2,1)}), bf16[128,8,768]{2,1,0:T(8,128)(2,1)}, u32[]{:S(2)}, u32[]{:S(2)}) async-start(bf16[128,8,768]{2,1,0:T(8,128)(2,1)} %fusion.9), calls=%async_computation | async-start | bytes 3145728 | tf_op jit(solution)/shard_map/all_to_all | solution.py:67
  84.5 0.0 collective-permute-done
  84.5 4.2 %multiply_reduce_fusion = (f32[]{:T(128)}, f32[768,768]{1,0:T(8,128)}) fusion(f32[768,768]{1,0:T(8,128)S(1)} %fusion.16, f32[768,768]{1,0:T(8,128)} %collective-permute-done), kind=kLoop, calls=%fused_computation.6 | loop fusion | flops 1769471 | bytes 7077892 | tf_op jit(solution)/shard_map/reduce_sum | solution.py:59
  89.3 6.1 %subtract_convert_fusion.2 = bf16[768,768]{1,0:T(8,128)(2,1)S(1)} fusion(f32[768,768]{1,0:T(8,128)} %get-tuple-element.8, f32[]{:T(128)S(6)} %mul_shard_map.3), kind=kOutput, calls=%fused_computation.4 | convolution fusion | flops 1819017216 | bytes 3538948 | tf_op jit(solution)/shard_map/dot_general | solution.py:37
  95.4 2.1 subtract_convert_fusion.1
  97.5 2.1 subtract_convert_fusion
  99.7 28.1 %all-to-all-done = bf16[128,8,768]{2,1,0:T(8,128)(2,1)} async-done(((bf16[128,8,768]{2,1,0:T(8,128)(2,1)}), bf16[128,8,768]{2,1,0:T(8,128)(2,1)}, u32[]{:S(2)}, u32[]{:S(2)}) %all-to-all-start) | async-done | bytes 1572896 | tf_op jit(solution)/shard_map/all_to_all | solution.py:67
  127.8 3.9 %fusion.10 = bf16[128,8,768]{2,1,0:T(8,128)(2,1)} fusion(bf16[768,768]{1,0:T(8,128)(2,1)S(1)} %subtract_convert_fusion, bf16[128,8,768]{2,1,0:T(8,128)(2,1)} %all-to-all-done), kind=kOutput, calls=%fused_computation.24 | convolution fusion | flops 1208745984 | bytes 4325376 | tf_op jit(solution)/shard_map/dot_general | solution.py:76
  131.7 6.7 %all-to-all-start.3 = ((bf16[128,8,768]{2,1,0:T(8,128)(2,1)}), bf16[128,8,768]{2,1,0:T(8,128)(2,1)S(1)}, u32[]{:S(2)}, u32[]{:S(2)}) async-start(bf16[128,8,768]{2,1,0:T(8,128)(2,1)} %fusion.10), calls=%async_computation.3 | async-start | bytes 3145728 | tf_op jit(solution)/shard_map/all_to_all | solution.py:77
  138.4 0.3 select_reduce_fusion
  138.7 41.6 %all-to-all-done.3 = bf16[128,8,768]{2,1,0:T(8,128)(2,1)S(1)} async-done(((bf16[128,8,768]{2,1,0:T(8,128)(2,1)}), bf16[128,8,768]{2,1,0:T(8,128)(2,1)S(1)}, u32[]{:S(2)}, u32[]{:S(2)}) %all-to-all-start.3) | async-done | bytes 1572896 | tf_op jit(solution)/shard_map/all_to_all | solution.py:77
  180.3 2.0 fusion.13
  182.3 46.5 %all_to_all.31 = bf16[128,8,768]{2,1,0:T(8,128)(2,1)S(1)} all-to-all(bf16[128,8,768]{2,1,0:T(8,128)(2,1)S(1)} %fusion.13), channel_id=1, replica_groups=mesh['docs'=128,'rep'=2] {'docs'}, dimensions={0} | all-to-all | bytes 3145728 | tf_op jit(solution)/shard_map/all_to_all | solution.py:82
  228.8 1.1 copy.10
  (2 shorter events, 0.0 us)
Async XLA Ops:
  0.0 71.2 %copy-start = (bf16[1,768,768]{2,1,0:T(8,128)(2,1)S(1)}, bf16[1,768,768]{2,1,0:T(8,128)(2,1)}, u32[]{:S(2)}) copy-start(bf16[1,768,768]{2,1,0:T(8,128)(2,1)} %param.10) | copy-start | bytes 3538948
  71.2 2.6 %copy-start.2 = (s32[512,1]{0,1:T(1,128)S(1)}, s32[512,1]{0,1:T(1,128)}, u32[]{:S(2)}) copy-start(s32[512,1]{0,1:T(1,128)} %param.8) | copy-start | bytes 6148
  71.2 2.6 %copy-start.3 = (s32[128]{0:T(128)S(1)}, s32[128]{0:T(128)}, u32[]{:S(2)}) copy-start(s32[128]{0:T(128)} %param.11) | copy-start | bytes 1540
  71.2 3.0 %copy-start.1 = (s32[512,1]{0,1:T(1,128)S(1)}, s32[512,1]{0,1:T(1,128)}, u32[]{:S(2)}) copy-start(s32[512,1]{0,1:T(1,128)} %param.7) | copy-start | bytes 6148
  71.2 3.4 %copy-start.4 = (bf16[512,768]{1,0:T(8,128)(2,1)S(1)}, bf16[512,768]{1,0:T(8,128)(2,1)}, u32[]{:S(2)}) copy-start(bf16[512,768]{1,0:T(8,128)(2,1)} %param.6) | copy-start | bytes 2359300
  73.7 10.7 %collective-permute-start = (f32[768,768]{1,0:T(8,128)S(1)}, f32[768,768]{1,0:T(8,128)}, u32[]{:S(2)}, u32[]{:S(2)}) collective-permute-start(f32[768,768]{1,0:T(8,128)S(1)} %fusion.16), channel_id=1, source_target_pairs={{0,1},{1,0},{2,3},{3,2},{4,5},{5,4},{6,7},{7,6},{8,9},{9,8},{10,11... | collective-permute-start | bytes 7077896 | tf_op jit(solution)/shard_map/ppermute | solution.py:58
  76.8 51.0 %all-to-all-start = ((bf16[128,8,768]{2,1,0:T(8,128)(2,1)}), bf16[128,8,768]{2,1,0:T(8,128)(2,1)}, u32[]{:S(2)}, u32[]{:S(2)}) async-start(bf16[128,8,768]{2,1,0:T(8,128)(2,1)} %fusion.9), calls=%async_computation | async-start | bytes 3145728 | tf_op jit(solution)/shard_map/all_to_all | solution.py:67
  131.7 48.6 %all-to-all-start.3 = ((bf16[128,8,768]{2,1,0:T(8,128)(2,1)}), bf16[128,8,768]{2,1,0:T(8,128)(2,1)S(1)}, u32[]{:S(2)}, u32[]{:S(2)}) async-start(bf16[128,8,768]{2,1,0:T(8,128)(2,1)} %fusion.10), calls=%async_computation.3 | async-start | bytes 3145728 | tf_op jit(solution)/shard_map/all_to_all | solution.py:77

commit v2 on v1

v2 whole, which is shorter than its diff:
```python
import math

import jax
import jax.numpy as jnp
from jax import lax
from jax.experimental import pallas as pl
from jax.experimental.pallas import tpu as pltpu
from jax.sharding import Mesh, PartitionSpec as P

ITERS = 3
DEPTH = 8
DOCS = ("x", "y", "z")


EPS = 1e-06
polar_scale = 0.3

bf16 = jnp.bfloat16
f32 = jnp.float32


def one_hot(targets, count):
    return jnp.arange(count, dtype=jnp.int32)[:, None] == targets[None, :]


def slot_ranks(labels, count):
    rows = labels.shape[0]
    onehot = (labels[:, None] == jnp.arange(count, dtype=jnp.int32)[None, :]).astype(bf16)
    order = jnp.arange(rows, dtype=jnp.int32)
    before = (order[None, :] < order[:, None]).astype(bf16)
    earlier = jnp.dot(before, onehot, preferred_element_type=f32)
    return jnp.sum(earlier * onehot.astype(f32), axis=1).astype(jnp.int32)


def select_rows(marks, rows):
    return jnp.dot(marks.astype(bf16), rows, preferred_element_type=f32).astype(bf16)


def fit_kernel(own_gram, rows, targets, rotation, gram, iterate, square):
    width = own_gram.shape[0]
    gram[...] = own_gram[...] + lax.dot_general(
        rows[...], targets[...], (((0,), (0,)), ((), ())), preferred_element_type=f32
    )
    total = jnp.sum(gram[...] * gram[...])
    factor = polar_scale * math.sqrt(width) * lax.rsqrt(total + EPS)
    iterate[...] = (gram[...] * factor).astype(bf16)
    for step in range(ITERS):
        square[...] = lax.dot_general(
            iterate[...], iterate[...], (((1,), (1,)), ((), ())), preferred_element_type=f32
        ).astype(bf16)
        update = jnp.dot(square[...], iterate[...], preferred_element_type=f32)
        later = (1.5 * iterate[...].astype(f32) - 0.5 * update).astype(bf16)
        if step < ITERS - 1:
            iterate[...] = later
        else:
            rotation[...] = later


def fit(own_gram, rows, targets):
    width = own_gram.shape[0]
    whole = pl.BlockSpec(memory_space=pltpu.VMEM)
    return pl.pallas_call(
        fit_kernel,
        out_shape=jax.ShapeDtypeStruct((width, width), bf16),
        in_specs=[whole] * 3,
        out_specs=whole,
        scratch_shapes=[
            pltpu.VMEM((width, width), f32),
            pltpu.VMEM((width, width), bf16),
            pltpu.VMEM((width, width), bf16),
        ],
        compiler_params=pltpu.CompilerParams(vmem_limit_bytes=32 * 2**20),
        cost_estimate=pl.CostEstimate(
            flops=2 * (rows.shape[0] * width**2 + 2 * ITERS * width**3), bytes_accessed=6 * 2**20, transcendentals=1
        ),
    )(own_gram, rows, targets)


def map_kernel(arrived, rotation, moved):
    moved[...] = jnp.dot(arrived[...], rotation[...], preferred_element_type=f32).astype(bf16)


def map_rows(arrived, rotation):
    rows, width = arrived.shape
    tile = rows // 4
    return pl.pallas_call(
        map_kernel,
        grid=(rows // tile,),
        out_shape=jax.ShapeDtypeStruct((rows, width), bf16),
        in_specs=[pl.BlockSpec((tile, width), lambda i: (i, 0)), pl.BlockSpec(memory_space=pltpu.VMEM)],
        out_specs=pl.BlockSpec((tile, width), lambda i: (i, 0)),
        compiler_params=pltpu.CompilerParams(vmem_limit_bytes=16 * 2**20),
        cost_estimate=pl.CostEstimate(flops=2 * rows * width**2, bytes_accessed=5 * 2**20, transcendentals=0),
    )(arrived, rotation)


def shards(slab, old_cluster, new_cluster, anchor_ids, anchor_new, owner_table):
    docs_count = lax.axis_size(DOCS)
    row_count, width = slab.shape
    capacity = 2 * row_count // docs_count
    slots = docs_count * capacity
    half = anchor_ids.shape[1]
    per_source = half // docs_count

    def exchange(x):
        return lax.all_to_all(x, DOCS, split_axis=0, concat_axis=0, tiled=True)

    def swap(x):
        return lax.ppermute(x, "rep", [(0, 1), (1, 0)])

    asked = exchange(anchor_ids.reshape(docs_count, per_source)).reshape(-1)
    picked = select_rows(asked[:, None] == jnp.arange(row_count, dtype=jnp.int32)[None, :], slab)
    fetched = exchange(picked.reshape(docs_count, per_source // 2, 2, width))
    other_new = swap(anchor_new[0])

    old_labels = old_cluster[:, 0]
    old_slot = old_labels * capacity + slot_ranks(old_labels, docs_count)
    outgoing = select_rows(one_hot(old_slot, slots), slab).reshape(docs_count, capacity, width)
    fetched, outgoing, other_new = lax.optimization_barrier((fetched, outgoing, other_new))
    arrived = exchange(outgoing).reshape(slots, width)

    fetched = fetched.reshape(half, width)
    other = swap(fetched)
    own_gram = jnp.einsum("ad,ae->de", fetched, anchor_new[0], preferred_element_type=f32)
    rotation = fit(own_gram, other, other_new)
    moved = map_rows(arrived, rotation)

    new_labels = new_cluster[:, 0]
    matches = new_labels[:, None] == jnp.arange(owner_table.shape[0], dtype=jnp.int32)[None, :]
    owners = jnp.sum(jnp.where(matches, owner_table[None, :], 0), axis=1)
    new_slot = owners * capacity + slot_ranks(new_labels, docs_count)
    source = jnp.sum(jnp.where(one_hot(new_slot, slots), old_slot[None, :] + 1, 0), axis=1) - 1

    returned = exchange(moved.reshape(docs_count, capacity, width)).reshape(slots, width)
    onward = select_rows(source[:, None] == jnp.arange(slots, dtype=jnp.int32)[None, :], returned)
    arrived_rows = exchange(onward.reshape(docs_count, capacity, width))
    return arrived_rows.reshape(1, slots, width)


def solution(mesh):
    docs_count, reps = mesh.devices.shape
    side = math.isqrt(docs_count // DEPTH)
    mesh = Mesh(mesh.devices.reshape(side, side, DEPTH, reps), DOCS + ("rep",))
    in_specs = (
        P(DOCS + ("rep",), None),
        P(DOCS + ("rep",), None),
        P(DOCS + ("rep",), None),
        P(DOCS, "rep"),
        P(DOCS, "rep", None),
        P(),
    )
    out_specs = P(DOCS, "rep", None)
    return jax.shard_map(shards, mesh=mesh, in_specs=in_specs, out_specs=out_specs, check_vma=False)
```

time: 230 us -> 213 us (0.926)
  blocking collectives: 112 us -> 68.1 us
  waiting for transfers between devices: 69.7 us -> 92.3 us
  matrix products: 23.5 us -> 8.37 us
  Pallas kernels: 0 us -> 9.52 us
  local copies, waits for them, and re-layouts: 3.69 us -> 11.4 us
  starting transfers between devices: 14.4 us -> 20.2 us
  other arithmetic: 6.21 us -> 1.99 us
    all_to_all x3 -> x2, blocking collectives: 112 us -> 68.1 us  [exchange(): return lax.all_to_all(x, DOCS, split_axis=0, concat_axis=0, tiled=True)]
    all_to_all x2 -> x3, waiting for transfers between devices: 69.7 us -> 91.9 us  [exchange(): return lax.all_to_all(x, DOCS, split_axis=0, concat_axis=0, tiled=True)]
    dot_general x5 -> x1, matrix products: 16.8 us -> 2.74 us  [shards(): jnp.einsum('ad,ae->de', fetched, anchor_new[0], preferred_element_type=f32)]
    pallas_call x0 -> x2, Pallas kernels: none -> 9.52 us  [the longest x1 7.58 us: fit(): pl.pallas_call(fit_kernel, out_shape=jax.ShapeDtypeStruct((width, width),...]
    all_to_all x2 -> x3, starting transfers between devices: 14.3 us -> 20.1 us  [exchange(): return lax.all_to_all(x, DOCS, split_axis=0, concat_axis=0, tiled=True)]
    unnamed x11 -> x17, local copies, waits for them, and re-layouts: 1.16 us -> 5.57 us
    reduce_sum x1 -> x0, other arithmetic: 4.2 us -> none  [shards(): jnp.sum(gram * gram) + EPS]
    reshape x2, local copies, waits for them, and re-layouts: 1.76 us -> 5.03 us  [the longest x1 3.74 us: shards(): fetched = fetched.reshape(half, width)]
  transfers between devices with their start and end apart: 3 -> 5, of which waited for: 2 -> 5; matrix products, arithmetic and copies ran while one was open for 8% -> 5% of each run, Pallas kernels for 0% -> 4%
where the time goes in v2:
time: 213 us; the launch traced here: 212 us
  waiting for transfers between devices  92.3 us (43%)
  blocking collectives  68.1 us (32%)
  starting transfers between devices  20.2 us (9%)
  local copies, waits for them, and re-layouts  11.4 us (5%)
  Pallas kernels  9.52 us (4%)
  matrix products  8.37 us (4%)
    all_to_all x3, waiting for transfers between devices, exchange(): return lax.all_to_all(x, DOCS, split_axis=0, concat_axis=0, tiled=True)  91.9 us
    all_to_all x2, blocking collectives, exchange(): return lax.all_to_all(x, DOCS, split_axis=0, concat_axis=0, tiled=True)  68.1 us
    all_to_all x3, starting transfers between devices, exchange(): return lax.all_to_all(x, DOCS, split_axis=0, concat_axis=0, tiled=True)  20.1 us
    pallas_call x1, Pallas kernels, fit(): pl.pallas_call(fit_kernel, out_shape=jax.ShapeDtypeStruct((width, width),...  7.58 us
    unnamed x17, local copies, waits for them, and re-layouts  5.57 us
    dot_general x3, matrix products, select_rows(): jnp.dot(marks.astype(bf16), rows, preferred_element_type=f32).astype(bf16)  5.01 us
  transfers between devices with their start and end apart: 5, of which 5 were waited for; matrix products, arithmetic and copies ran while one was open for 5% of the time, Pallas kernels for 4%

profile of v2, /device:TPU:32, one launch (start us, length us, event | category | flops | bytes accessed | tf_op | source)
XLA Modules:
  0.0 212.0 jit_solution(3927949518323786636)
XLA Ops:
  0.0 0.0 copy-start
  0.0 0.8 reduce
  0.8 0.1 all_to_all.18
  0.9 25.9 %all_to_all.29 = s32[128,1,6]{2,1,0:T(1,128)S(1)} all-to-all(s32[128,1,6]{2,1,0:T(1,128)S(1)} %bitcast.24), channel_id=1, replica_groups=mesh['x'=4,'y'=4,'z'=8,'rep'=2] {'x','y','z'}, dimensions={0} | all-to-all | bytes 6144 | tf_op jit(solution)/shard_map/all_to_all | solution.py:106
  26.9 0.5 broadcast.36
  27.4 0.8 reduce.4
  28.2 0.1 eq.102
  28.3 0.0 copy-done
  28.3 0.9 fusion.7
  29.2 1.3 reshape.57
  30.5 0.0 copy-start.6
  30.5 0.0 copy-start.7
  30.5 0.0 copy-start.5
  30.5 6.8 %all-to-all-start.1 = ((bf16[128,3,2,768]{3,2,1,0:T(2,128)(2,1)}), bf16[128,3,2,768]{3,2,1,0:T(2,128)(2,1)S(1)}, u32[]{:S(2)}, u32[]{:S(2)}) async-start(bf16[128,3,2,768]{3,2,1,0:T(2,128)(2,1)} %reshape.57), calls=%async_computation.1 | async-start | bytes 2359296 | tf_op jit(solution)/shard_map/all_to_all | solution.py:106
  37.3 0.1 collective-permute-start
  37.4 0.0 copy-done.6
  37.4 0.0 copy-done.7
  37.4 0.1 select_reduce_fusion.1
  37.5 0.3 fusion.12
  37.8 0.0 copy-done.5
  37.8 0.3 fusion.13
  38.2 2.2 %fusion.8 = bf16[128,8,768]{2,1,0:T(8,128)(2,1)} fusion(bf16[512,768]{1,0:T(8,128)(2,1)S(1)} %copy-done, s32[512]{0:T(512)S(1)} %get-tuple-element.12), kind=kOutput, calls=%fused_computation.13 | convolution fusion | flops 806617088 | bytes 2361344 | tf_op jit(solution)/shard_map/dot_general | solution.py:36
  40.3 0.1 collective-permute-done.targets
  40.4 30.0 %all-to-all-done.1 = bf16[128,3,2,768]{3,2,1,0:T(2,128)(2,1)S(1)} async-done(((bf16[128,3,2,768]{3,2,1,0:T(2,128)(2,1)}), bf16[128,3,2,768]{3,2,1,0:T(2,128)(2,1)S(1)}, u32[]{:S(2)}, u32[]{:S(2)}) %all-to-all-start.1) | async-done | bytes 1179680 | tf_op jit(solution)/shard_map/all_to_all | solution.py:106
  70.4 0.0 copy-start.4
  70.4 1.0 copy-done.4
  71.4 6.7 %all-to-all-start.2 = ((bf16[128,8,768]{2,1,0:T(8,128)(2,1)}), bf16[128,8,768]{2,1,0:T(8,128)(2,1)S(1)}, u32[]{:S(2)}, u32[]{:S(2)}) async-start(bf16[128,8,768]{2,1,0:T(8,128)(2,1)} %fusion.8), calls=%async_computation.2 | async-start | bytes 3145728 | tf_op jit(solution)/shard_map/all_to_all | solution.py:106
  78.1 3.7 %reshape.60 = bf16[768,768]{1,0:T(8,128)(2,1)} reshape(bf16[128,3,2,768]{3,2,1,0:T(2,128)(2,1)} %copy-done.4) | data formatting | bytes 2359296 | tf_op jit(solution)/shard_map/reshape | solution.py:122
  81.8 0.0 collective-permute-start.1
  81.8 2.7 %fusion.20.own_gram = f32[768,768]{1,0:T(8,128)S(1)} fusion(bf16[768,768]{1,0:T(8,128)(2,1)} %reshape.60, bf16[1,768,768]{2,1,0:T(8,128)(2,1)} %param.10), kind=kOutput, calls=%fused_computation.33 | convolution fusion | flops 905969664 | bytes 4718592 | tf_op jit(solution)/shard_map/ad,ae->de/dot_general | solution.py:124
  84.6 0.3 collective-permute-done.1.rows
  84.9 7.6 %shard_map.64.rotation = bf16[768,768]{1,0:T(8,128)(2,1)S(1)} custom-call(f32[768,768]{1,0:T(8,128)S(1)} %fusion.20.own_gram, bf16[768,768]{1,0:T(8,128)(2,1)S(1)} %collective-permute-done.1.rows, bf16[768,768]{1,0:T(8,128)(2,1)S(1)} %collective-permute-done.targets), custom_call_target="tpu_custom_call" | custom-call | flops 6341787648 | bytes 6291456 | tf_op jit(solution)/shard_map/pallas_call | solution.py:62
  92.5 0.0 copy-start.2
  92.5 1.0 copy-done.2
  93.5 24.3 %all-to-all-done.2 = bf16[128,8,768]{2,1,0:T(8,128)(2,1)S(1)} async-done(((bf16[128,8,768]{2,1,0:T(8,128)(2,1)}), bf16[128,8,768]{2,1,0:T(8,128)(2,1)S(1)}, u32[]{:S(2)}, u32[]{:S(2)}) %all-to-all-start.2) | async-done | bytes 1572896 | tf_op jit(solution)/shard_map/all_to_all | solution.py:106
  117.8 0.0 copy-start.3
  117.8 1.3 copy-done.3
  119.1 1.9 shard_map.65
  121.0 0.0 copy-start.1
  121.0 1.1 copy-done.1
  122.1 6.7 %all-to-all-start.3 = ((bf16[128,8,768]{2,1,0:T(8,128)(2,1)}), bf16[128,8,768]{2,1,0:T(8,128)(2,1)S(1)}, u32[]{:S(2)}, u32[]{:S(2)}) async-start(bf16[128,8,768]{2,1,0:T(8,128)(2,1)} %bitcast.22), calls=%async_computation.3 | async-start | bytes 3145728 | tf_op jit(solution)/shard_map/all_to_all | solution.py:106
  128.8 0.3 select_reduce_fusion
  129.1 37.6 %all-to-all-done.3 = bf16[128,8,768]{2,1,0:T(8,128)(2,1)S(1)} async-done(((bf16[128,8,768]{2,1,0:T(8,128)(2,1)}), bf16[128,8,768]{2,1,0:T(8,128)(2,1)S(1)}, u32[]{:S(2)}, u32[]{:S(2)}) %all-to-all-start.3) | async-done | bytes 1572896 | tf_op jit(solution)/shard_map/all_to_all | solution.py:106
  166.7 2.0 fusion.9
  168.7 42.1 %all_to_all.30 = bf16[128,8,768]{2,1,0:T(8,128)(2,1)S(1)} all-to-all(bf16[128,8,768]{2,1,0:T(8,128)(2,1)S(1)} %fusion.9), channel_id=1, replica_groups=mesh['x'=4,'y'=4,'z'=8,'rep'=2] {'x','y','z'}, dimensions={0} | all-to-all | bytes 3145728 | tf_op jit(solution)/shard_map/all_to_all | solution.py:106
  210.9 1.1 copy.10
  (2 shorter events, 0.0 us)
Async XLA Ops:
  0.0 28.3 %copy-start = (bf16[512,768]{1,0:T(8,128)(2,1)S(1)}, bf16[512,768]{1,0:T(8,128)(2,1)}, u32[]{:S(2)}) copy-start(bf16[512,768]{1,0:T(8,128)(2,1)} %param.6) | copy-start | bytes 2359300
  30.5 6.9 %copy-start.6 = (s32[512,1]{0,1:T(1,128)S(1)}, s32[512,1]{0,1:T(1,128)}, u32[]{:S(2)}) copy-start(s32[512,1]{0,1:T(1,128)} %param.8) | copy-start | bytes 6148
  30.5 6.9 %copy-start.7 = (s32[128]{0:T(128)S(1)}, s32[128]{0:T(128)}, u32[]{:S(2)}) copy-start(s32[128]{0:T(128)} %param.11) | copy-start | bytes 1540
  30.5 7.3 %copy-start.5 = (s32[512,1]{0,1:T(1,128)S(1)}, s32[512,1]{0,1:T(1,128)}, u32[]{:S(2)}) copy-start(s32[512,1]{0,1:T(1,128)} %param.7) | copy-start | bytes 6148
  30.5 39.9 %all-to-all-start.1 = ((bf16[128,3,2,768]{3,2,1,0:T(2,128)(2,1)}), bf16[128,3,2,768]{3,2,1,0:T(2,128)(2,1)S(1)}, u32[]{:S(2)}, u32[]{:S(2)}) async-start(bf16[128,3,2,768]{3,2,1,0:T(2,128)(2,1)} %reshape.57), calls=%async_computation.1 | async-start | bytes 2359296 | tf_op jit(solution)/shard_map/all_to_all | solution.py:106
  37.3 3.1 %collective-permute-start = (bf16[768,768]{1,0:T(8,128)(2,1)}, bf16[768,768]{1,0:T(8,128)(2,1)S(1)}, u32[]{:S(2)}, u32[]{:S(2)}) collective-permute-start(bf16[768,768]{1,0:T(8,128)(2,1)} %bitcast.29), channel_id=1, source_target_pairs={{0,1},{1,0},{2,3},{3,2},{4,5},{5,4},{6,7},{7,6},{8,9},{9,8},{10,11... | collective-permute-start | bytes 3538952 | tf_op jit(solution)/shard_map/ppermute | solution.py:109
  70.4 1.0 copy-start.4
  71.4 46.4 %all-to-all-start.2 = ((bf16[128,8,768]{2,1,0:T(8,128)(2,1)}), bf16[128,8,768]{2,1,0:T(8,128)(2,1)S(1)}, u32[]{:S(2)}, u32[]{:S(2)}) async-start(bf16[128,8,768]{2,1,0:T(8,128)(2,1)} %fusion.8), calls=%async_computation.2 | async-start | bytes 3145728 | tf_op jit(solution)/shard_map/all_to_all | solution.py:106
  81.8 3.1 %collective-permute-start.1 = (bf16[768,768]{1,0:T(8,128)(2,1)}, bf16[768,768]{1,0:T(8,128)(2,1)S(1)}, u32[]{:S(2)}, u32[]{:S(2)}) collective-permute-start(bf16[768,768]{1,0:T(8,128)(2,1)} %reshape.60), channel_id=1, source_target_pairs={{0,1},{1,0},{2,3},{3,2},{4,5},{5,4},{6,7},{7,6},{8,9},{9,8},{10,11... | collective-permute-start | bytes 3538952 | tf_op jit(solution)/shard_map/ppermute | solution.py:109
  92.5 1.0 copy-start.2
  117.8 1.3 copy-start.3
  121.0 1.1 copy-start.1
  122.1 44.6 %all-to-all-start.3 = ((bf16[128,8,768]{2,1,0:T(8,128)(2,1)}), bf16[128,8,768]{2,1,0:T(8,128)(2,1)S(1)}, u32[]{:S(2)}, u32[]{:S(2)}) async-start(bf16[128,8,768]{2,1,0:T(8,128)(2,1)} %bitcast.22), calls=%async_computation.3 | async-start | bytes 3145728 | tf_op jit(solution)/shard_map/all_to_all | solution.py:106

commit v3 on v2

--- a/solution.py
+++ b/solution.py
@@ -10,6 +10,9 @@
 ITERS = 3
 DEPTH = 8
 DOCS = ("x", "y", "z")
+TILES = 4
+HEAD_START = 3
+MAP_PASSES = 4
 
 
 EPS = 1e-06
@@ -17,19 +20,6 @@
 
 bf16 = jnp.bfloat16
 f32 = jnp.float32
-
-
-def one_hot(targets, count):
-    return jnp.arange(count, dtype=jnp.int32)[:, None] == targets[None, :]
-
-
-def slot_ranks(labels, count):
-    rows = labels.shape[0]
-    onehot = (labels[:, None] == jnp.arange(count, dtype=jnp.int32)[None, :]).astype(bf16)
-    order = jnp.arange(rows, dtype=jnp.int32)
-    before = (order[None, :] < order[:, None]).astype(bf16)
-    earlier = jnp.dot(before, onehot, preferred_element_type=f32)
-    return jnp.sum(earlier * onehot.astype(f32), axis=1).astype(jnp.int32)
 
 
 def select_rows(marks, rows):
@@ -76,22 +66,93 @@
     )(own_gram, rows, targets)
 
 
-def map_kernel(arrived, rotation, moved):
-    moved[...] = jnp.dot(arrived[...], rotation[...], preferred_element_type=f32).astype(bf16)
-
-
-def map_rows(arrived, rotation):
+def map_kernel(passes, arrived, rotation, moved):
+    @pl.loop(0, passes[0])
+    def _(_):
+        moved[...] = jnp.dot(arrived[...], rotation[...], preferred_element_type=f32).astype(bf16)
+
+
+def map_rows(passes, arrived, rotation):
     rows, width = arrived.shape
-    tile = rows // 4
+    tile = rows // TILES
     return pl.pallas_call(
         map_kernel,
-        grid=(rows // tile,),
-        out_shape=jax.ShapeDtypeStruct((rows, width), bf16),
-        in_specs=[pl.BlockSpec((tile, width), lambda i: (i, 0)), pl.BlockSpec(memory_space=pltpu.VMEM)],
+        grid=(TILES,),
+        out_shape=pltpu.HBM((rows, width), bf16),
+        in_specs=[
+            pl.BlockSpec(memory_space=pltpu.SMEM),
+            pl.BlockSpec((tile, width), lambda i: (i, 0)),
+            pl.BlockSpec((width, width), lambda i: (0, 0)),
+        ],
         out_specs=pl.BlockSpec((tile, width), lambda i: (i, 0)),
-        compiler_params=pltpu.CompilerParams(vmem_limit_bytes=16 * 2**20),
+        compiler_params=pltpu.CompilerParams(vmem_limit_bytes=12 * 2**20),
         cost_estimate=pl.CostEstimate(flops=2 * rows * width**2, bytes_accessed=5 * 2**20, transcendentals=0),
-    )(arrived, rotation)
+    )(passes.reshape(1), arrived, rotation)
+
+
+def prepare_kernel(
+    turn, old_labels, new_labels, owner_of, slab, *refs
+):
+    outgoing, selection, rows_out, selection_out, row_sems, selection_sems = refs[-6:]
+    rows = slab.shape[0]
+    count = owner_of.shape[0]
+    slots = outgoing.shape[0]
+    capacity = slots // count
+    tile = slots // TILES
+
+    @pl.loop(0, turn[0])
+    def _(_):
+        def ints(shape, axis):
+            return lax.broadcasted_iota(jnp.int32, shape, axis)
+
+        earlier = jnp.where(ints((rows, rows), 0) < ints((rows, rows), 1), 1.0, 0.0).astype(bf16)
+        names = ints((count, rows), 0)
+
+        def rank(labels):
+            named = names == labels
+            before = jnp.dot(jnp.where(named, 1.0, 0.0).astype(bf16), earlier, preferred_element_type=f32)
+            return jnp.sum(jnp.where(named, before, 0.0), axis=0, keepdims=True)
+
+        old, new = old_labels[...], new_labels[...]
+        owners = jnp.sum(jnp.where(names == new, owner_of[...].astype(f32), 0.0), axis=0, keepdims=True)
+        old_slot = old * capacity + rank(old).astype(jnp.int32)
+        new_slot = owners.astype(jnp.int32) * capacity + rank(new).astype(jnp.int32)
+        copies = []
+        for i in range(TILES):
+            part = pl.ds(i * tile, tile)
+            here = ints((tile, rows), 0) + i * tile
+            marks = jnp.where(here == old_slot, 1.0, 0.0).astype(bf16)
+            rows_out[i] = jnp.dot(marks, slab[...], preferred_element_type=f32).astype(bf16)
+            copies.append(pltpu.make_async_copy(rows_out.at[i], outgoing.at[part], row_sems.at[i]))
+            copies[-1].start()
+            source = jnp.sum(jnp.where(here == new_slot, (old_slot + 1).astype(f32), 0.0), axis=1, keepdims=True) - 1.0
+            chosen = ints((tile, slots), 1) == source.astype(jnp.int32)
+            selection_out[i] = jnp.where(chosen, 1.0, 0.0).astype(bf16)
+            copies.append(pltpu.make_async_copy(selection_out.at[i], selection.at[part], selection_sems.at[i]))
+            copies[-1].start()
+        for copy in copies:
+            copy.wait()
+
+
+def prepare(turn, old_labels, new_labels, owner_table, slab, slots, held=None):
+    rows, width = slab.shape
+    near, far = pl.BlockSpec(memory_space=pltpu.VMEM), pl.BlockSpec(memory_space=pltpu.HBM)
+    held = () if held is None else held
+    return pl.pallas_call(
+        prepare_kernel,
+        out_shape=[pltpu.HBM((slots, width), bf16), pltpu.HBM((slots, slots), bf16)],
+        in_specs=[pl.BlockSpec(memory_space=pltpu.SMEM)] + [near] * 4 + [far] * len(held),
+        out_specs=[far, far],
+        input_output_aliases={5 + i: i for i in range(len(held))},
+        scratch_shapes=[
+            pltpu.VMEM((TILES, slots // TILES, width), bf16),
+            pltpu.VMEM((TILES, slots // TILES, slots), bf16),
+            pltpu.SemaphoreType.DMA((TILES,)),
+            pltpu.SemaphoreType.DMA((TILES,)),
+        ],
+        compiler_params=pltpu.CompilerParams(vmem_limit_bytes=24 * 2**20),
+        cost_estimate=pl.CostEstimate(flops=2 * slots * rows * width, bytes_accessed=5 * 2**20, transcendentals=0),
+    )(turn.reshape(1), old_labels, new_labels, owner_table[:, None], slab, *held)
 
 
 def shards(slab, old_cluster, new_cluster, anchor_ids, anchor_new, owner_table):
@@ -101,6 +162,8 @@
     slots = docs_count * capacity
     half = anchor_ids.shape[1]
     per_source = half // docs_count
+    core = lax.axis_index("rep")
+    local = (old_cluster.reshape(1, row_count), new_cluster.reshape(1, row_count), owner_table, slab, slots)
 
     def exchange(x):
         return lax.all_to_all(x, DOCS, split_axis=0, concat_axis=0, tiled=True)
@@ -108,31 +171,25 @@
     def swap(x):
         return lax.ppermute(x, "rep", [(0, 1), (1, 0)])
 
+    held = prepare(jnp.where(core == 0, HEAD_START, 0), *local)
+    anchor_ids, held = lax.optimization_barrier((anchor_ids, held))
     asked = exchange(anchor_ids.reshape(docs_count, per_source)).reshape(-1)
     picked = select_rows(asked[:, None] == jnp.arange(row_count, dtype=jnp.int32)[None, :], slab)
+    picked, held = lax.optimization_barrier((picked, held))
     fetched = exchange(picked.reshape(docs_count, per_source // 2, 2, width))
     other_new = swap(anchor_new[0])
-
-    old_labels = old_cluster[:, 0]
-    old_slot = old_labels * capacity + slot_ranks(old_labels, docs_count)
-    outgoing = select_rows(one_hot(old_slot, slots), slab).reshape(docs_count, capacity, width)
+    outgoing, selection = prepare(jnp.where(core == 0, 0, 1), *local, held)
     fetched, outgoing, other_new = lax.optimization_barrier((fetched, outgoing, other_new))
-    arrived = exchange(outgoing).reshape(slots, width)
+    arrived = exchange(outgoing.reshape(docs_count, capacity, width)).reshape(slots, width)
 
     fetched = fetched.reshape(half, width)
     other = swap(fetched)
     own_gram = jnp.einsum("ad,ae->de", fetched, anchor_new[0], preferred_element_type=f32)
     rotation = fit(own_gram, other, other_new)
-    moved = map_rows(arrived, rotation)
-
-    new_labels = new_cluster[:, 0]
-    matches = new_labels[:, None] == jnp.arange(owner_table.shape[0], dtype=jnp.int32)[None, :]
-    owners = jnp.sum(jnp.where(matches, owner_table[None, :], 0), axis=1)
-    new_slot = owners * capacity + slot_ranks(new_labels, docs_count)
-    source = jnp.sum(jnp.where(one_hot(new_slot, slots), old_slot[None, :] + 1, 0), axis=1) - 1
+    moved = map_rows(jnp.where(core == 0, MAP_PASSES, 1), arrived, rotation)
 
     returned = exchange(moved.reshape(docs_count, capacity, width)).reshape(slots, width)
-    onward = select_rows(source[:, None] == jnp.arange(slots, dtype=jnp.int32)[None, :], returned)
+    onward = select_rows(selection, returned)
     arrived_rows = exchange(onward.reshape(docs_count, capacity, width))
     return arrived_rows.reshape(1, slots, width)
 

time: 213 us -> 196 us (0.920)
  waiting for transfers between devices: 92.3 us -> 40.7 us
  blocking collectives: 68.1 us -> 95.7 us
  Pallas kernels: 9.52 us -> 25.2 us
  starting transfers between devices: 20.2 us -> 14.4 us
  matrix products: 8.37 us -> 5.4 us
    all_to_all x3 -> x2, waiting for transfers between devices: 91.9 us -> 37.4 us  [exchange(): return lax.all_to_all(x, DOCS, split_axis=0, concat_axis=0, tiled=True)]
    all_to_all x2 -> x3, blocking collectives: 68.1 us -> 95.7 us  [exchange(): return lax.all_to_all(x, DOCS, split_axis=0, concat_axis=0, tiled=True)]
    pallas_call x1 -> x3, Pallas kernels: 1.94 us -> 16.4 us  [the longest x1 8.47 us: map_rows(): pl.pallas_call(map_kernel, grid=(TILES,), out_shape=pltpu.HBM((rows, widt...]
    all_to_all x3 -> x2, starting transfers between devices: 20.1 us -> 14.3 us  [exchange(): return lax.all_to_all(x, DOCS, split_axis=0, concat_axis=0, tiled=True)]
    ppermute x2, waiting for transfers between devices: 0.38 us -> 3.36 us  [swap(): return lax.ppermute(x, 'rep', [(0, 1), (1, 0)])]
    dot_general x3 -> x2, matrix products: 5.01 us -> 2.65 us  [select_rows(): jnp.dot(marks.astype(bf16), rows, preferred_element_type=f32).astype(bf16)]
    unnamed x17 -> x21, local copies, waits for them, and re-layouts: 5.57 us -> 5.93 us
  transfers between devices with their start and end apart: 5 -> 4, of which waited for: 5 -> 4; matrix products, arithmetic and copies ran while one was open for 5% -> 3% of each run, Pallas kernels for 4% -> 5%
where the time goes in v3:
time: 196 us; the launch traced here: 195 us
  blocking collectives  95.7 us (49%)
  waiting for transfers between devices  40.7 us (21%)
  Pallas kernels  25.2 us (13%)
  starting transfers between devices  14.4 us (7%)
  local copies, waits for them, and re-layouts  12.5 us (6%)
  matrix products  5.4 us (3%)
    all_to_all x3, blocking collectives, exchange(): return lax.all_to_all(x, DOCS, split_axis=0, concat_axis=0, tiled=True)  95.7 us
    all_to_all x2, waiting for transfers between devices, exchange(): return lax.all_to_all(x, DOCS, split_axis=0, concat_axis=0, tiled=True)  37.4 us
    all_to_all x2, starting transfers between devices, exchange(): return lax.all_to_all(x, DOCS, split_axis=0, concat_axis=0, tiled=True)  14.3 us
    pallas_call x1, Pallas kernels, fit(): pl.pallas_call(fit_kernel, out_shape=jax.ShapeDtypeStruct((width, width),...  8.85 us
    pallas_call x1, Pallas kernels, map_rows(): pl.pallas_call(map_kernel, grid=(TILES,), out_shape=pltpu.HBM((rows, widt...  8.47 us
    pallas_call x2, Pallas kernels, prepare(): pl.pallas_call(prepare_kernel, out_shape=[pltpu.HBM((slots, width), bf16)...  7.9 us
    unnamed x21, local copies, waits for them, and re-layouts  5.93 us
  transfers between devices with their start and end apart: 4, of which 4 were waited for; matrix products, arithmetic and copies ran while one was open for 3% of the time, Pallas kernels for 5%

profile of v3, /device:TPU:32, one launch (start us, length us, event | category | flops | bytes accessed | tf_op | source)
XLA Modules:
  0.0 194.8 jit_solution(11433459297453939045)
XLA Ops:
  0.0 0.0 copy-start.9
  0.0 0.8 copy.15.owner_of
  0.8 0.0 copy-start
  0.8 1.1 copy-done
  1.9 0.0 copy-start.2
  1.9 0.7 copy-done.2
  2.6 0.0 copy-start.4
  2.6 0.7 copy-done.4
  3.3 0.0 copy-start.1
  3.3 7.8 %shard_map.64 = (bf16[1024,768]{1,0:T(8,128)(2,1)}, bf16[1024,1024]{1,0:T(8,128)(2,1)}) custom-call(s32[1]{0:T(128)} %bitcast.4.turn, s32[1,512]{1,0:T(1,128)S(1)} %bitcast.25, s32[1,512]{1,0:T(1,128)S(1)} %bitcast.27, s32[128,1]{1,0:T(8,128)S(1)} %copy.15.owner_of, bf16[512,768]{1,0:T(8,128)(2,1)S(1)} %copy-done), custom_call_target="tpu_custom_call" | custom-call | flops 805306368 | bytes 5242880 | tf_op jit(solution)/shard_map/pallas_call | solution.py:141
  11.1 0.0 copy-done.9
  11.1 0.1 all_to_all.18
  11.3 25.9 %all_to_all.29 = s32[128,1,6]{2,1,0:T(1,128)S(1)} all-to-all(s32[128,1,6]{2,1,0:T(1,128)S(1)} %bitcast.32), channel_id=1, replica_groups=mesh['x'=4,'y'=4,'z'=8,'rep'=2] {'x','y','z'}, dimensions={0} | all-to-all | bytes 6144 | tf_op jit(solution)/shard_map/all_to_all | solution.py:169
  37.2 0.5 broadcast.4
  37.7 0.7 reduce.4
  38.4 0.1 eq.21
  38.6 0.0 copy-done.1
  38.6 0.9 fusion.2
  39.4 1.3 reshape.50
  40.7 0.0 copy-start.3
  40.7 0.0 copy-start.5
  40.7 7.8 %all-to-all-start.1 = ((bf16[128,3,2,768]{3,2,1,0:T(2,128)(2,1)}), bf16[128,3,2,768]{3,2,1,0:T(2,128)(2,1)}, u32[]{:S(2)}, u32[]{:S(2)}) async-start(bf16[128,3,2,768]{3,2,1,0:T(2,128)(2,1)} %reshape.50), calls=%async_computation.1 | async-start | bytes 2359296 | tf_op jit(solution)/shard_map/all_to_all | solution.py:169
  48.5 0.1 collective-permute-start
  48.6 0.0 copy-done.3
  48.6 0.0 copy-done.5
  48.6 0.1 shard_map.65
  48.7 2.9 %collective-permute-done.targets = bf16[768,768]{1,0:T(8,128)(2,1)S(1)} collective-permute-done((bf16[768,768]{1,0:T(8,128)(2,1)}, bf16[768,768]{1,0:T(8,128)(2,1)S(1)}, u32[]{:S(2)}, u32[]{:S(2)}) %collective-permute-start) | collective-permute-done | bytes 1179680 | tf_op jit(solution)/shard_map/ppermute | solution.py:172
  51.6 22.0 %all-to-all-done.1 = bf16[128,3,2,768]{3,2,1,0:T(2,128)(2,1)} async-done(((bf16[128,3,2,768]{3,2,1,0:T(2,128)(2,1)}), bf16[128,3,2,768]{3,2,1,0:T(2,128)(2,1)}, u32[]{:S(2)}, u32[]{:S(2)}) %all-to-all-start.1) | async-done | bytes 1179680 | tf_op jit(solution)/shard_map/all_to_all | solution.py:169
  73.7 6.6 %all-to-all-start.2 = ((bf16[128,8,768]{2,1,0:T(8,128)(2,1)}), bf16[128,8,768]{2,1,0:T(8,128)(2,1)S(1)}, u32[]{:S(2)}, u32[]{:S(2)}) async-start(bf16[128,8,768]{2,1,0:T(8,128)(2,1)} %bitcast.30), calls=%async_computation.2 | async-start | bytes 3145728 | tf_op jit(solution)/shard_map/all_to_all | solution.py:169
  80.3 3.7 %reshape.53 = bf16[768,768]{1,0:T(8,128)(2,1)} reshape(bf16[128,3,2,768]{3,2,1,0:T(2,128)(2,1)} %all-to-all-done.1) | data formatting | bytes 2359296 | tf_op jit(solution)/shard_map/reshape | solution.py:185
  84.0 0.0 collective-permute-start.1
  84.0 2.7 %fusion.7.own_gram = f32[768,768]{1,0:T(8,128)S(1)} fusion(bf16[768,768]{1,0:T(8,128)(2,1)} %reshape.53, bf16[1,768,768]{2,1,0:T(8,128)(2,1)} %param.10), kind=kOutput, calls=%fused_computation.7 | convolution fusion | flops 905969664 | bytes 4718592 | tf_op jit(solution)/shard_map/ad,ae->de/dot_general | solution.py:187
  86.8 0.4 collective-permute-done.1.rows
  87.2 8.8 %shard_map.66.rotation = bf16[768,768]{1,0:T(8,128)(2,1)S(1)} custom-call(f32[768,768]{1,0:T(8,128)S(1)} %fusion.7.own_gram, bf16[768,768]{1,0:T(8,128)(2,1)} %collective-permute-done.1.rows, bf16[768,768]{1,0:T(8,128)(2,1)S(1)} %collective-permute-done.targets), custom_call_target="tpu_custom_call" | custom-call | flops 6341787648 | bytes 6291456 | tf_op jit(solution)/shard_map/pallas_call | solution.py:52
  96.0 0.0 copy-start.6
  96.1 1.0 copy-done.6
  97.1 15.3 %all-to-all-done.2 = bf16[128,8,768]{2,1,0:T(8,128)(2,1)S(1)} async-done(((bf16[128,8,768]{2,1,0:T(8,128)(2,1)}), bf16[128,8,768]{2,1,0:T(8,128)(2,1)S(1)}, u32[]{:S(2)}, u32[]{:S(2)}) %all-to-all-start.2) | async-done | bytes 1572896 | tf_op jit(solution)/shard_map/all_to_all | solution.py:169
  112.4 0.0 copy-start.7
  112.4 1.3 copy-done.7
  113.7 8.5 %shard_map.67 = bf16[1024,768]{1,0:T(8,128)(2,1)} custom-call(s32[1]{0:T(128)} %bitcast.6.passes, bf16[1024,768]{1,0:T(8,128)(2,1)S(1)} %bitcast.24, bf16[768,768]{1,0:T(8,128)(2,1)S(1)} %copy-done.7), custom_call_target="tpu_custom_call" | custom-call | flops 1207959552 | bytes 5242880 | tf_op jit(solution)/shard_map/pallas_call | solution.py:78
  122.1 0.0 copy-start.8
  122.1 36.1 %all_to_all.30 = bf16[128,8,768]{2,1,0:T(8,128)(2,1)S(1)} all-to-all(bf16[128,8,768]{2,1,0:T(8,128)(2,1)} %bitcast.31), channel_id=1, replica_groups=mesh['x'=4,'y'=4,'z'=8,'rep'=2] {'x','y','z'}, dimensions={0} | all-to-all | bytes 3145728 | tf_op jit(solution)/shard_map/all_to_all | solution.py:169
  158.3 0.0 copy-done.8
  158.3 1.8 fusion.3
  160.1 33.6 %all_to_all.31 = bf16[128,8,768]{2,1,0:T(8,128)(2,1)S(1)} all-to-all(bf16[128,8,768]{2,1,0:T(8,128)(2,1)S(1)} %fusion.3), channel_id=1, replica_groups=mesh['x'=4,'y'=4,'z'=8,'rep'=2] {'x','y','z'}, dimensions={0} | all-to-all | bytes 3145728 | tf_op jit(solution)/shard_map/all_to_all | solution.py:169
  193.7 1.1 copy.19
  (1 shorter events, 0.0 us)
Async XLA Ops:
  0.0 11.1 %copy-start.9 = (s32[1,768]{1,0:T(1,128)S(1)}, s32[1,768]{1,0:T(1,128)}, u32[]{:S(2)}) copy-start(s32[1,768]{1,0:T(1,128)} %param.9) | copy-start | bytes 9220
  0.8 1.1 copy-start
  1.9 0.7 copy-start.2
  2.6 0.7 copy-start.4
  3.3 35.3 %copy-start.1 = (bf16[512,768]{1,0:T(8,128)(2,1)S(1)}, bf16[512,768]{1,0:T(8,128)(2,1)}, u32[]{:S(2)}) copy-start(bf16[512,768]{1,0:T(8,128)(2,1)} %slab.3) | copy-start | bytes 2359300
  40.7 7.9 %copy-start.3 = (s32[512,1]{0,1:T(1,128)S(1)}, s32[512,1]{0,1:T(1,128)}, u32[]{:S(2)}) copy-start(s32[512,1]{0,1:T(1,128)} %param.7) | copy-start | bytes 6148
  40.7 7.9 %copy-start.5 = (s32[512,1]{0,1:T(1,128)S(1)}, s32[512,1]{0,1:T(1,128)}, u32[]{:S(2)}) copy-start(s32[512,1]{0,1:T(1,128)} %param.8) | copy-start | bytes 6148
  40.7 33.0 %all-to-all-start.1 = ((bf16[128,3,2,768]{3,2,1,0:T(2,128)(2,1)}), bf16[128,3,2,768]{3,2,1,0:T(2,128)(2,1)}, u32[]{:S(2)}, u32[]{:S(2)}) async-start(bf16[128,3,2,768]{3,2,1,0:T(2,128)(2,1)} %reshape.50), calls=%async_computation.1 | async-start | bytes 2359296 | tf_op jit(solution)/shard_map/all_to_all | solution.py:169
  48.5 3.1 %collective-permute-start = (bf16[768,768]{1,0:T(8,128)(2,1)}, bf16[768,768]{1,0:T(8,128)(2,1)S(1)}, u32[]{:S(2)}, u32[]{:S(2)}) collective-permute-start(bf16[768,768]{1,0:T(8,128)(2,1)} %bitcast.34), channel_id=1, source_target_pairs={{0,1},{1,0},{2,3},{3,2},{4,5},{5,4},{6,7},{7,6},{8,9},{9,8},{10,11... | collective-permute-start | bytes 3538952 | tf_op jit(solution)/shard_map/ppermute | solution.py:172
  73.7 38.7 %all-to-all-start.2 = ((bf16[128,8,768]{2,1,0:T(8,128)(2,1)}), bf16[128,8,768]{2,1,0:T(8,128)(2,1)S(1)}, u32[]{:S(2)}, u32[]{:S(2)}) async-start(bf16[128,8,768]{2,1,0:T(8,128)(2,1)} %bitcast.30), calls=%async_computation.2 | async-start | bytes 3145728 | tf_op jit(solution)/shard_map/all_to_all | solution.py:169
  84.0 3.2 %collective-permute-start.1 = (bf16[768,768]{1,0:T(8,128)(2,1)}, bf16[768,768]{1,0:T(8,128)(2,1)}, u32[]{:S(2)}, u32[]{:S(2)}) collective-permute-start(bf16[768,768]{1,0:T(8,128)(2,1)} %reshape.53), channel_id=1, source_target_pairs={{0,1},{1,0},{2,3},{3,2},{4,5},{5,4},{6,7},{7,6},{8,9},{9,8},{10,11... | collective-permute-start | bytes 3538952 | tf_op jit(solution)/shard_map/ppermute | solution.py:172
  96.0 1.0 copy-start.6
  112.4 1.3 copy-start.7
  122.1 36.1 %copy-start.8 = (bf16[1024,1024]{1,0:T(8,128)(2,1)S(1)}, bf16[1024,1024]{1,0:T(8,128)(2,1)}, u32[]{:S(2)}) copy-start(bf16[1024,1024]{1,0:T(8,128)(2,1)} %get-tuple-element.25) | copy-start | bytes 6291460

commit v4 on v3

--- a/solution.py
+++ b/solution.py
@@ -11,8 +11,8 @@
 DEPTH = 8
 DOCS = ("x", "y", "z")
 TILES = 4
-HEAD_START = 3
-MAP_PASSES = 4
+HEAD_START = 2
+MAP_PASSES = 2
 
 
 EPS = 1e-06
@@ -90,33 +90,46 @@
     )(passes.reshape(1), arrived, rotation)
 
 
-def prepare_kernel(
-    turn, old_labels, new_labels, owner_of, slab, *refs
-):
-    outgoing, selection, rows_out, selection_out, row_sems, selection_sems = refs[-6:]
+def prepare_kernel(turn, old_ref, new_ref, owner_ref, slab_ref, *refs):
+    outgoing, selection, old_row, new_row, owner_of, slab, rows_out, selection_out, fetch_sems, row_sems, selection_sems = refs[-11:]
     rows = slab.shape[0]
-    count = owner_of.shape[0]
+    count = owner_of.shape[1]
     slots = outgoing.shape[0]
     capacity = slots // count
     tile = slots // TILES
 
     @pl.loop(0, turn[0])
     def _(_):
+        fetches = [
+            pltpu.make_async_copy(source, target, fetch_sems.at[i])
+            for i, (source, target) in enumerate(
+                ((old_ref, old_row), (new_ref, new_row), (owner_ref, owner_of), (slab_ref, slab))
+            )
+        ]
+        for fetch in fetches:
+            fetch.start()
+        for fetch in fetches:
+            fetch.wait()
+
         def ints(shape, axis):
             return lax.broadcasted_iota(jnp.int32, shape, axis)
 
         earlier = jnp.where(ints((rows, rows), 0) < ints((rows, rows), 1), 1.0, 0.0).astype(bf16)
         names = ints((count, rows), 0)
 
-        def rank(labels):
-            named = names == labels
-            before = jnp.dot(jnp.where(named, 1.0, 0.0).astype(bf16), earlier, preferred_element_type=f32)
-            return jnp.sum(jnp.where(named, before, 0.0), axis=0, keepdims=True)
-
-        old, new = old_labels[...], new_labels[...]
-        owners = jnp.sum(jnp.where(names == new, owner_of[...].astype(f32), 0.0), axis=0, keepdims=True)
-        old_slot = old * capacity + rank(old).astype(jnp.int32)
-        new_slot = owners.astype(jnp.int32) * capacity + rank(new).astype(jnp.int32)
+        def named(labels):
+            return jnp.where(names == labels, 1.0, 0.0)
+
+        def rank(marks):
+            before = jnp.dot(marks.astype(bf16), earlier, preferred_element_type=f32)
+            return jnp.sum(marks * before, axis=0, keepdims=True).astype(jnp.int32)
+
+        old, new = old_row[...], new_row[...]
+        old_marks, new_marks = named(old), named(new)
+        table = jnp.broadcast_to(owner_of[...].astype(f32), (8, count)).astype(bf16)
+        owners = jnp.dot(table, new_marks.astype(bf16), preferred_element_type=f32)[:1].astype(jnp.int32)
+        old_slot = old * capacity + rank(old_marks)
+        new_slot = owners * capacity + rank(new_marks)
         copies = []
         for i in range(TILES):
             part = pl.ds(i * tile, tile)
@@ -134,25 +147,30 @@
             copy.wait()
 
 
-def prepare(turn, old_labels, new_labels, owner_table, slab, slots, held=None):
+def prepare(turn, old_labels, new_labels, owner_table, slab, slots, held=()):
     rows, width = slab.shape
-    near, far = pl.BlockSpec(memory_space=pltpu.VMEM), pl.BlockSpec(memory_space=pltpu.HBM)
-    held = () if held is None else held
+    count = owner_table.shape[0]
+    far = pl.BlockSpec(memory_space=pl.ANY)
     return pl.pallas_call(
         prepare_kernel,
         out_shape=[pltpu.HBM((slots, width), bf16), pltpu.HBM((slots, slots), bf16)],
-        in_specs=[pl.BlockSpec(memory_space=pltpu.SMEM)] + [near] * 4 + [far] * len(held),
-        out_specs=[far, far],
+        in_specs=[pl.BlockSpec(memory_space=pltpu.SMEM)] + [far] * (4 + len(held)),
+        out_specs=[pl.BlockSpec(memory_space=pltpu.HBM)] * 2,
         input_output_aliases={5 + i: i for i in range(len(held))},
         scratch_shapes=[
+            pltpu.VMEM((1, rows), jnp.int32),
+            pltpu.VMEM((1, rows), jnp.int32),
+            pltpu.VMEM((1, count), jnp.int32),
+            pltpu.VMEM((rows, width), bf16),
             pltpu.VMEM((TILES, slots // TILES, width), bf16),
             pltpu.VMEM((TILES, slots // TILES, slots), bf16),
+            pltpu.SemaphoreType.DMA((4,)),
             pltpu.SemaphoreType.DMA((TILES,)),
             pltpu.SemaphoreType.DMA((TILES,)),
         ],
-        compiler_params=pltpu.CompilerParams(vmem_limit_bytes=24 * 2**20),
+        compiler_params=pltpu.CompilerParams(vmem_limit_bytes=60 * 2**20),
         cost_estimate=pl.CostEstimate(flops=2 * slots * rows * width, bytes_accessed=5 * 2**20, transcendentals=0),
-    )(turn.reshape(1), old_labels, new_labels, owner_table[:, None], slab, *held)
+    )(turn.reshape(1), old_labels, new_labels, owner_table.reshape(1, count), slab, *held)
 
 
 def shards(slab, old_cluster, new_cluster, anchor_ids, anchor_new, owner_table):
@@ -176,13 +194,12 @@
     asked = exchange(anchor_ids.reshape(docs_count, per_source)).reshape(-1)
     picked = select_rows(asked[:, None] == jnp.arange(row_count, dtype=jnp.int32)[None, :], slab)
     picked, held = lax.optimization_barrier((picked, held))
-    fetched = exchange(picked.reshape(docs_count, per_source // 2, 2, width))
+    fetched = exchange(picked.reshape(docs_count, per_source // 2, 2, width)).reshape(half, width)
     other_new = swap(anchor_new[0])
     outgoing, selection = prepare(jnp.where(core == 0, 0, 1), *local, held)
     fetched, outgoing, other_new = lax.optimization_barrier((fetched, outgoing, other_new))
     arrived = exchange(outgoing.reshape(docs_count, capacity, width)).reshape(slots, width)
 
-    fetched = fetched.reshape(half, width)
     other = swap(fetched)
     own_gram = jnp.einsum("ad,ae->de", fetched, anchor_new[0], preferred_element_type=f32)
     rotation = fit(own_gram, other, other_new)

time: 196 us -> 190 us (0.969)
  local copies, waits for them, and re-layouts: 12.5 us -> 6.86 us
  waiting for transfers between devices: 40.7 us -> 45.6 us
  Pallas kernels: 25.2 us -> 21.3 us
    all_to_all x2, waiting for transfers between devices: 37.4 us -> 45.1 us  [exchange(): return lax.all_to_all(x, DOCS, split_axis=0, concat_axis=0, tiled=True)]
    pallas_call x1, Pallas kernels: 8.47 us -> 4.64 us  [map_rows(): pl.pallas_call(map_kernel, grid=(TILES,), out_shape=pltpu.HBM((rows, widt...]
    ppermute x2, waiting for transfers between devices: 3.36 us -> 0.42 us  [swap(): return lax.ppermute(x, 'rep', [(0, 1), (1, 0)])]
    unnamed x21 -> x13, local copies, waits for them, and re-layouts: 5.93 us -> 3.44 us
    reshape x2, local copies, waits for them, and re-layouts: 5.03 us -> 2.59 us  [the longest x1 1.31 us: shards(): picked.reshape(docs_count, per_source // 2, 2, width)]
  transfers between devices with their start and end apart: 4 -> 4, of which waited for: 4 -> 3; matrix products, arithmetic and copies ran while one was open for 3% -> 2% of each run, Pallas kernels for 5% -> 5%
where the time goes in v4:
time: 190 us
  blocking collectives  95.7 us (50%)
  waiting for transfers between devices  45.6 us (24%)
  Pallas kernels  21.3 us (11%)
  starting transfers between devices  13.8 us (7%)
  local copies, waits for them, and re-layouts  6.86 us (4%)
  matrix products  5.4 us (3%)
    all_to_all x3, blocking collectives, exchange(): return lax.all_to_all(x, DOCS, split_axis=0, concat_axis=0, tiled=True)  95.7 us
    all_to_all x2, waiting for transfers between devices, exchange(): return lax.all_to_all(x, DOCS, split_axis=0, concat_axis=0, tiled=True)  45.1 us
    all_to_all x2, starting transfers between devices, exchange(): return lax.all_to_all(x, DOCS, split_axis=0, concat_axis=0, tiled=True)  13.4 us
    pallas_call x1, Pallas kernels, fit(): pl.pallas_call(fit_kernel, out_shape=jax.ShapeDtypeStruct((width, width),...  8.85 us
    pallas_call x2, Pallas kernels, prepare(): pl.pallas_call(prepare_kernel, out_shape=[pltpu.HBM((slots, width), bf16)...  7.85 us
    pallas_call x1, Pallas kernels, map_rows(): pl.pallas_call(map_kernel, grid=(TILES,), out_shape=pltpu.HBM((rows, widt...  4.64 us
  transfers between devices with their start and end apart: 4, of which 3 were waited for; matrix products, arithmetic and copies ran while one was open for 2% of the time, Pallas kernels for 5%

profile of v4, /device:TPU:32, one launch (start us, length us, event | category | flops | bytes accessed | tf_op | source)
XLA Modules:
  0.0 189.6 jit_solution(5867333421666540847)
XLA Ops:
  0.0 0.0 copy-start.4
  0.0 0.0 copy-start.3
  0.0 7.7 %shard_map.64 = (bf16[1024,768]{1,0:T(8,128)(2,1)}, bf16[1024,1024]{1,0:T(8,128)(2,1)}) custom-call(s32[1]{0:T(128)} %bitcast.4.turn, s32[1,512]{1,0:T(1,128)} %bitcast.29, s32[1,512]{1,0:T(1,128)} %bitcast.31, s32[1,128]{1,0:T(1,128)} %bitcast.33, bf16[512,768]{1,0:T(8,128)(2,1)} %slab_ref.3), custom_call_target="tpu_custom_call" | custom-call | flops 805306368 | bytes 5242880 | tf_op jit(solution)/shard_map/pallas_call | solution.py:154
  7.7 0.0 copy-done.4
  7.8 0.1 all_to_all.18
  7.9 25.9 %all_to_all.29 = s32[128,1,6]{2,1,0:T(1,128)S(1)} all-to-all(s32[128,1,6]{2,1,0:T(1,128)S(1)} %bitcast.28), channel_id=1, replica_groups=mesh['x'=4,'y'=4,'z'=8,'rep'=2] {'x','y','z'}, dimensions={0} | all-to-all | bytes 6144 | tf_op jit(solution)/shard_map/all_to_all | solution.py:187
  33.9 0.6 broadcast.4
  34.4 0.8 reduce.4
  35.2 0.1 eq.21
  35.4 0.0 copy-done.3
  35.4 0.9 fusion.2
  36.3 1.3 reshape.55
  37.6 0.0 copy-start.5
  37.6 6.8 %all-to-all-start.1 = ((bf16[128,3,2,768]{3,2,1,0:T(2,128)(2,1)}), bf16[128,3,2,768]{3,2,1,0:T(2,128)(2,1)S(1)}, u32[]{:S(2)}, u32[]{:S(2)}) async-start(bf16[128,3,2,768]{3,2,1,0:T(2,128)(2,1)} %reshape.55), calls=%async_computation.1 | async-start | bytes 2359296 | tf_op jit(solution)/shard_map/all_to_all | solution.py:187
  44.4 0.0 copy-done.5
  44.4 0.1 collective-permute-start
  44.5 0.1 shard_map.65
  44.6 25.8 %all-to-all-done.1 = bf16[128,3,2,768]{3,2,1,0:T(2,128)(2,1)S(1)} async-done(((bf16[128,3,2,768]{3,2,1,0:T(2,128)(2,1)}), bf16[128,3,2,768]{3,2,1,0:T(2,128)(2,1)S(1)}, u32[]{:S(2)}, u32[]{:S(2)}) %all-to-all-start.1) | async-done | bytes 1179680 | tf_op jit(solution)/shard_map/all_to_all | solution.py:187
  70.4 1.3 reshape.56
  71.7 0.0 collective-permute-done.targets
  71.7 6.7 %all-to-all-start.2 = ((bf16[128,8,768]{2,1,0:T(8,128)(2,1)}), bf16[128,8,768]{2,1,0:T(8,128)(2,1)S(1)}, u32[]{:S(2)}, u32[]{:S(2)}) async-start(bf16[128,8,768]{2,1,0:T(8,128)(2,1)} %bitcast.25), calls=%async_computation.2 | async-start | bytes 3145728 | tf_op jit(solution)/shard_map/all_to_all | solution.py:187
  78.4 0.3 collective-permute-start.1
  78.6 2.7 %fusion.7.own_gram = f32[768,768]{1,0:T(8,128)S(1)} fusion(bf16[768,768]{1,0:T(8,128)(2,1)} %reshape.56, bf16[1,768,768]{2,1,0:T(8,128)(2,1)} %param.10), kind=kOutput, calls=%fused_computation.7 | convolution fusion | flops 905969664 | bytes 4718592 | tf_op jit(solution)/shard_map/ad,ae->de/dot_general | solution.py:204
  81.4 0.4 collective-permute-done.1.rows
  81.8 8.8 %shard_map.66.rotation = bf16[768,768]{1,0:T(8,128)(2,1)S(1)} custom-call(f32[768,768]{1,0:T(8,128)S(1)} %fusion.7.own_gram, bf16[768,768]{1,0:T(8,128)(2,1)} %collective-permute-done.1.rows, bf16[768,768]{1,0:T(8,128)(2,1)S(1)} %collective-permute-done.targets), custom_call_target="tpu_custom_call" | custom-call | flops 6341787648 | bytes 6291456 | tf_op jit(solution)/shard_map/pallas_call | solution.py:52
  90.7 0.0 copy-start
  90.7 1.0 copy-done
  91.7 19.3 %all-to-all-done.2 = bf16[128,8,768]{2,1,0:T(8,128)(2,1)S(1)} async-done(((bf16[128,8,768]{2,1,0:T(8,128)(2,1)}), bf16[128,8,768]{2,1,0:T(8,128)(2,1)S(1)}, u32[]{:S(2)}, u32[]{:S(2)}) %all-to-all-start.2) | async-done | bytes 1572896 | tf_op jit(solution)/shard_map/all_to_all | solution.py:187
  111.0 0.0 copy-start.1
  111.0 1.3 copy-done.1
  112.3 4.6 %shard_map.67 = bf16[1024,768]{1,0:T(8,128)(2,1)} custom-call(s32[1]{0:T(128)} %bitcast.6.passes, bf16[1024,768]{1,0:T(8,128)(2,1)S(1)} %bitcast.24, bf16[768,768]{1,0:T(8,128)(2,1)S(1)} %copy-done.1), custom_call_target="tpu_custom_call" | custom-call | flops 1207959552 | bytes 5242880 | tf_op jit(solution)/shard_map/pallas_call | solution.py:78
  116.9 0.0 copy-start.2
  116.9 36.1 %all_to_all.30 = bf16[128,8,768]{2,1,0:T(8,128)(2,1)S(1)} all-to-all(bf16[128,8,768]{2,1,0:T(8,128)(2,1)} %bitcast.27), channel_id=1, replica_groups=mesh['x'=4,'y'=4,'z'=8,'rep'=2] {'x','y','z'}, dimensions={0} | all-to-all | bytes 3145728 | tf_op jit(solution)/shard_map/all_to_all | solution.py:187
  153.0 0.0 copy-done.2
  153.0 1.8 fusion.3
  154.8 33.6 %all_to_all.31 = bf16[128,8,768]{2,1,0:T(8,128)(2,1)S(1)} all-to-all(bf16[128,8,768]{2,1,0:T(8,128)(2,1)S(1)} %fusion.3), channel_id=1, replica_groups=mesh['x'=4,'y'=4,'z'=8,'rep'=2] {'x','y','z'}, dimensions={0} | all-to-all | bytes 3145728 | tf_op jit(solution)/shard_map/all_to_all | solution.py:187
  188.5 1.1 copy.13
  (1 shorter events, 0.0 us)
Async XLA Ops:
  0.0 7.8 %copy-start.4 = (s32[1,768]{1,0:T(1,128)S(1)}, s32[1,768]{1,0:T(1,128)}, u32[]{:S(2)}) copy-start(s32[1,768]{1,0:T(1,128)} %param.9) | copy-start | bytes 9220
  0.0 35.4 %copy-start.3 = (bf16[512,768]{1,0:T(8,128)(2,1)S(1)}, bf16[512,768]{1,0:T(8,128)(2,1)}, u32[]{:S(2)}) copy-start(bf16[512,768]{1,0:T(8,128)(2,1)} %slab_ref.3) | copy-start | bytes 2359300
  37.6 6.8 %copy-start.5 = (bf16[1,768,768]{2,1,0:T(8,128)(2,1)S(1)}, bf16[1,768,768]{2,1,0:T(8,128)(2,1)}, u32[]{:S(2)}) copy-start(bf16[1,768,768]{2,1,0:T(8,128)(2,1)} %param.10) | copy-start | bytes 3538948
  37.6 32.8 %all-to-all-start.1 = ((bf16[128,3,2,768]{3,2,1,0:T(2,128)(2,1)}), bf16[128,3,2,768]{3,2,1,0:T(2,128)(2,1)S(1)}, u32[]{:S(2)}, u32[]{:S(2)}) async-start(bf16[128,3,2,768]{3,2,1,0:T(2,128)(2,1)} %reshape.55), calls=%async_computation.1 | async-start | bytes 2359296 | tf_op jit(solution)/shard_map/all_to_all | solution.py:187
  44.4 27.3 %collective-permute-start = (bf16[768,768]{1,0:T(8,128)(2,1)S(1)}, bf16[768,768]{1,0:T(8,128)(2,1)S(1)}, u32[]{:S(2)}, u32[]{:S(2)}) collective-permute-start(bf16[768,768]{1,0:T(8,128)(2,1)S(1)} %bitcast.35), channel_id=1, source_target_pairs={{0,1},{1,0},{2,3},{3,2},{4,5},{5,4},{6,7},{7,6},{8,9},{9,8},{10,11... | collective-permute-start | bytes 3538952 | tf_op jit(solution)/shard_map/ppermute | solution.py:190
  71.7 39.3 %all-to-all-start.2 = ((bf16[128,8,768]{2,1,0:T(8,128)(2,1)}), bf16[128,8,768]{2,1,0:T(8,128)(2,1)S(1)}, u32[]{:S(2)}, u32[]{:S(2)}) async-start(bf16[128,8,768]{2,1,0:T(8,128)(2,1)} %bitcast.25), calls=%async_computation.2 | async-start | bytes 3145728 | tf_op jit(solution)/shard_map/all_to_all | solution.py:187
  78.4 3.5 %collective-permute-start.1 = (bf16[768,768]{1,0:T(8,128)(2,1)}, bf16[768,768]{1,0:T(8,128)(2,1)}, u32[]{:S(2)}, u32[]{:S(2)}) collective-permute-start(bf16[768,768]{1,0:T(8,128)(2,1)} %reshape.56), channel_id=1, source_target_pairs={{0,1},{1,0},{2,3},{3,2},{4,5},{5,4},{6,7},{7,6},{8,9},{9,8},{10,11... | collective-permute-start | bytes 3538952 | tf_op jit(solution)/shard_map/ppermute | solution.py:190
  90.7 1.0 copy-start
  111.0 1.3 copy-start.1
  116.9 36.1 %copy-start.2 = (bf16[1024,1024]{1,0:T(8,128)(2,1)S(1)}, bf16[1024,1024]{1,0:T(8,128)(2,1)}, u32[]{:S(2)}) copy-start(bf16[1024,1024]{1,0:T(8,128)(2,1)} %get-tuple-element.25) | copy-start | bytes 6291460

commit v5 on v4

--- a/solution.py
+++ b/solution.py
@@ -74,10 +74,10 @@
 
 def map_rows(passes, arrived, rotation):
     rows, width = arrived.shape
-    tile = rows // TILES
+    tile = rows // 2
     return pl.pallas_call(
         map_kernel,
-        grid=(TILES,),
+        grid=(2,),
         out_shape=pltpu.HBM((rows, width), bf16),
         in_specs=[
             pl.BlockSpec(memory_space=pltpu.SMEM),
@@ -85,7 +85,7 @@
             pl.BlockSpec((width, width), lambda i: (0, 0)),
         ],
         out_specs=pl.BlockSpec((tile, width), lambda i: (i, 0)),
-        compiler_params=pltpu.CompilerParams(vmem_limit_bytes=12 * 2**20),
+        compiler_params=pltpu.CompilerParams(vmem_limit_bytes=24 * 2**20),
         cost_estimate=pl.CostEstimate(flops=2 * rows * width**2, bytes_accessed=5 * 2**20, transcendentals=0),
     )(passes.reshape(1), arrived, rotation)
 

time: 190 us -> 190 us (level)
  no operation moved by 1% of the time
where the time goes in v5:
time: 190 us; the launch traced here: 189 us
  blocking collectives  95.9 us (50%)
  waiting for transfers between devices  45.6 us (24%)
  Pallas kernels  20.7 us (11%)
  starting transfers between devices  13.8 us (7%)
  local copies, waits for them, and re-layouts  6.86 us (4%)
  matrix products  5.4 us (3%)
    all_to_all x3, blocking collectives, exchange(): return lax.all_to_all(x, DOCS, split_axis=0, concat_axis=0, tiled=True)  95.9 us
    all_to_all x2, waiting for transfers between devices, exchange(): return lax.all_to_all(x, DOCS, split_axis=0, concat_axis=0, tiled=True)  45.1 us
    all_to_all x2, starting transfers between devices, exchange(): return lax.all_to_all(x, DOCS, split_axis=0, concat_axis=0, tiled=True)  13.4 us
    pallas_call x1, Pallas kernels, fit(): pl.pallas_call(fit_kernel, out_shape=jax.ShapeDtypeStruct((width, width),...  8.85 us
    pallas_call x2, Pallas kernels, prepare(): pl.pallas_call(prepare_kernel, out_shape=[pltpu.HBM((slots, width), bf16)...  7.85 us
    pallas_call x1, Pallas kernels, map_rows(): pl.pallas_call(map_kernel, grid=(2,), out_shape=pltpu.HBM((rows, width),...  4.02 us
  transfers between devices with their start and end apart: 4, of which 3 were waited for; matrix products, arithmetic and copies ran while one was open for 2% of the time, Pallas kernels for 5%

profile of v5, /device:TPU:32, one launch (start us, length us, event | category | flops | bytes accessed | tf_op | source)
XLA Modules:
  0.0 189.2 jit_solution(9752799107250694086)
XLA Ops:
  0.0 0.0 copy-start.4
  0.0 0.0 copy-start.3
  0.0 7.7 %shard_map.64 = (bf16[1024,768]{1,0:T(8,128)(2,1)}, bf16[1024,1024]{1,0:T(8,128)(2,1)}) custom-call(s32[1]{0:T(128)} %bitcast.4.turn, s32[1,512]{1,0:T(1,128)} %bitcast.29, s32[1,512]{1,0:T(1,128)} %bitcast.31, s32[1,128]{1,0:T(1,128)} %bitcast.33, bf16[512,768]{1,0:T(8,128)(2,1)} %slab_ref.3), custom_call_target="tpu_custom_call" | custom-call | flops 805306368 | bytes 5242880 | tf_op jit(solution)/shard_map/pallas_call | solution.py:154
  7.7 0.0 copy-done.4
  7.8 0.1 all_to_all.18
  7.9 25.9 %all_to_all.29 = s32[128,1,6]{2,1,0:T(1,128)S(1)} all-to-all(s32[128,1,6]{2,1,0:T(1,128)S(1)} %bitcast.28), channel_id=1, replica_groups=mesh['x'=4,'y'=4,'z'=8,'rep'=2] {'x','y','z'}, dimensions={0} | all-to-all | bytes 6144 | tf_op jit(solution)/shard_map/all_to_all | solution.py:187
  33.9 0.6 broadcast.4
  34.4 0.8 reduce.4
  35.2 0.1 eq.21
  35.4 0.0 copy-done.3
  35.4 0.9 fusion.2
  36.3 1.3 reshape.55
  37.6 0.0 copy-start.5
  37.6 6.8 %all-to-all-start.1 = ((bf16[128,3,2,768]{3,2,1,0:T(2,128)(2,1)}), bf16[128,3,2,768]{3,2,1,0:T(2,128)(2,1)S(1)}, u32[]{:S(2)}, u32[]{:S(2)}) async-start(bf16[128,3,2,768]{3,2,1,0:T(2,128)(2,1)} %reshape.55), calls=%async_computation.1 | async-start | bytes 2359296 | tf_op jit(solution)/shard_map/all_to_all | solution.py:187
  44.4 0.0 copy-done.5
  44.4 0.1 collective-permute-start
  44.5 0.1 shard_map.65
  44.6 25.8 %all-to-all-done.1 = bf16[128,3,2,768]{3,2,1,0:T(2,128)(2,1)S(1)} async-done(((bf16[128,3,2,768]{3,2,1,0:T(2,128)(2,1)}), bf16[128,3,2,768]{3,2,1,0:T(2,128)(2,1)S(1)}, u32[]{:S(2)}, u32[]{:S(2)}) %all-to-all-start.1) | async-done | bytes 1179680 | tf_op jit(solution)/shard_map/all_to_all | solution.py:187
  70.4 1.3 reshape.56
  71.7 0.0 collective-permute-done.targets
  71.7 6.7 %all-to-all-start.2 = ((bf16[128,8,768]{2,1,0:T(8,128)(2,1)}), bf16[128,8,768]{2,1,0:T(8,128)(2,1)S(1)}, u32[]{:S(2)}, u32[]{:S(2)}) async-start(bf16[128,8,768]{2,1,0:T(8,128)(2,1)} %bitcast.25), calls=%async_computation.2 | async-start | bytes 3145728 | tf_op jit(solution)/shard_map/all_to_all | solution.py:187
  78.4 0.3 collective-permute-start.1
  78.6 2.7 %fusion.7.own_gram = f32[768,768]{1,0:T(8,128)S(1)} fusion(bf16[768,768]{1,0:T(8,128)(2,1)} %reshape.56, bf16[1,768,768]{2,1,0:T(8,128)(2,1)} %param.10), kind=kOutput, calls=%fused_computation.7 | convolution fusion | flops 905969664 | bytes 4718592 | tf_op jit(solution)/shard_map/ad,ae->de/dot_general | solution.py:204
  81.4 0.4 collective-permute-done.1.rows
  81.8 8.8 %shard_map.66.rotation = bf16[768,768]{1,0:T(8,128)(2,1)S(1)} custom-call(f32[768,768]{1,0:T(8,128)S(1)} %fusion.7.own_gram, bf16[768,768]{1,0:T(8,128)(2,1)} %collective-permute-done.1.rows, bf16[768,768]{1,0:T(8,128)(2,1)S(1)} %collective-permute-done.targets), custom_call_target="tpu_custom_call" | custom-call | flops 6341787648 | bytes 6291456 | tf_op jit(solution)/shard_map/pallas_call | solution.py:52
  90.7 0.0 copy-start
  90.7 1.0 copy-done
  91.7 19.3 %all-to-all-done.2 = bf16[128,8,768]{2,1,0:T(8,128)(2,1)S(1)} async-done(((bf16[128,8,768]{2,1,0:T(8,128)(2,1)}), bf16[128,8,768]{2,1,0:T(8,128)(2,1)S(1)}, u32[]{:S(2)}, u32[]{:S(2)}) %all-to-all-start.2) | async-done | bytes 1572896 | tf_op jit(solution)/shard_map/all_to_all | solution.py:187
  111.0 0.0 copy-start.1
  111.0 1.3 copy-done.1
  112.3 4.0 %shard_map.67 = bf16[1024,768]{1,0:T(8,128)(2,1)} custom-call(s32[1]{0:T(128)} %bitcast.6.passes, bf16[1024,768]{1,0:T(8,128)(2,1)S(1)} %bitcast.24, bf16[768,768]{1,0:T(8,128)(2,1)S(1)} %copy-done.1), custom_call_target="tpu_custom_call" | custom-call | flops 1207959552 | bytes 5242880 | tf_op jit(solution)/shard_map/pallas_call | solution.py:78
  116.3 0.0 copy-start.2
  116.3 36.3 %all_to_all.30 = bf16[128,8,768]{2,1,0:T(8,128)(2,1)S(1)} all-to-all(bf16[128,8,768]{2,1,0:T(8,128)(2,1)} %bitcast.27), channel_id=1, replica_groups=mesh['x'=4,'y'=4,'z'=8,'rep'=2] {'x','y','z'}, dimensions={0} | all-to-all | bytes 3145728 | tf_op jit(solution)/shard_map/all_to_all | solution.py:187
  152.6 0.0 copy-done.2
  152.6 1.8 fusion.3
  154.4 33.7 %all_to_all.31 = bf16[128,8,768]{2,1,0:T(8,128)(2,1)S(1)} all-to-all(bf16[128,8,768]{2,1,0:T(8,128)(2,1)S(1)} %fusion.3), channel_id=1, replica_groups=mesh['x'=4,'y'=4,'z'=8,'rep'=2] {'x','y','z'}, dimensions={0} | all-to-all | bytes 3145728 | tf_op jit(solution)/shard_map/all_to_all | solution.py:187
  188.1 1.1 copy.13
  (1 shorter events, 0.0 us)
Async XLA Ops:
  0.0 7.8 %copy-start.4 = (s32[1,768]{1,0:T(1,128)S(1)}, s32[1,768]{1,0:T(1,128)}, u32[]{:S(2)}) copy-start(s32[1,768]{1,0:T(1,128)} %param.9) | copy-start | bytes 9220
  0.0 35.4 %copy-start.3 = (bf16[512,768]{1,0:T(8,128)(2,1)S(1)}, bf16[512,768]{1,0:T(8,128)(2,1)}, u32[]{:S(2)}) copy-start(bf16[512,768]{1,0:T(8,128)(2,1)} %slab_ref.3) | copy-start | bytes 2359300
  37.6 6.8 %copy-start.5 = (bf16[1,768,768]{2,1,0:T(8,128)(2,1)S(1)}, bf16[1,768,768]{2,1,0:T(8,128)(2,1)}, u32[]{:S(2)}) copy-start(bf16[1,768,768]{2,1,0:T(8,128)(2,1)} %param.10) | copy-start | bytes 3538948
  37.6 32.8 %all-to-all-start.1 = ((bf16[128,3,2,768]{3,2,1,0:T(2,128)(2,1)}), bf16[128,3,2,768]{3,2,1,0:T(2,128)(2,1)S(1)}, u32[]{:S(2)}, u32[]{:S(2)}) async-start(bf16[128,3,2,768]{3,2,1,0:T(2,128)(2,1)} %reshape.55), calls=%async_computation.1 | async-start | bytes 2359296 | tf_op jit(solution)/shard_map/all_to_all | solution.py:187
  44.4 27.3 %collective-permute-start = (bf16[768,768]{1,0:T(8,128)(2,1)S(1)}, bf16[768,768]{1,0:T(8,128)(2,1)S(1)}, u32[]{:S(2)}, u32[]{:S(2)}) collective-permute-start(bf16[768,768]{1,0:T(8,128)(2,1)S(1)} %bitcast.35), channel_id=1, source_target_pairs={{0,1},{1,0},{2,3},{3,2},{4,5},{5,4},{6,7},{7,6},{8,9},{9,8},{10,11... | collective-permute-start | bytes 3538952 | tf_op jit(solution)/shard_map/ppermute | solution.py:190
  71.7 39.3 %all-to-all-start.2 = ((bf16[128,8,768]{2,1,0:T(8,128)(2,1)}), bf16[128,8,768]{2,1,0:T(8,128)(2,1)S(1)}, u32[]{:S(2)}, u32[]{:S(2)}) async-start(bf16[128,8,768]{2,1,0:T(8,128)(2,1)} %bitcast.25), calls=%async_computation.2 | async-start | bytes 3145728 | tf_op jit(solution)/shard_map/all_to_all | solution.py:187
  78.4 3.5 %collective-permute-start.1 = (bf16[768,768]{1,0:T(8,128)(2,1)}, bf16[768,768]{1,0:T(8,128)(2,1)}, u32[]{:S(2)}, u32[]{:S(2)}) collective-permute-start(bf16[768,768]{1,0:T(8,128)(2,1)} %reshape.56), channel_id=1, source_target_pairs={{0,1},{1,0},{2,3},{3,2},{4,5},{5,4},{6,7},{7,6},{8,9},{9,8},{10,11... | collective-permute-start | bytes 3538952 | tf_op jit(solution)/shard_map/ppermute | solution.py:190
  90.7 1.0 copy-start
  111.0 1.3 copy-start.1
  116.3 36.3 %copy-start.2 = (bf16[1024,1024]{1,0:T(8,128)(2,1)S(1)}, bf16[1024,1024]{1,0:T(8,128)(2,1)}, u32[]{:S(2)}) copy-start(bf16[1024,1024]{1,0:T(8,128)(2,1)} %get-tuple-element.25) | copy-start | bytes 6291460
